TPU v7x, 128 devices: a whole 4x4x4 slice. The times are simulated.
128 devices in a mesh: visit: 16 (over y_hi, x, core), strip: 8 (over y_lo, z).
Axes of the slice: x: 4, y: 4 (y_hi: 2, y_lo: 2; y = y_hi * 2 + y_lo), z: 4, core: 2. Of those that a mesh axis runs over, the one named last changes fastest.
Arguments:
- science: float32 [32, 512, 4096], P('visit', 'strip'), may hold values from -6 to 6
- template: float32 [512, 4096], P('strip', 'visit'), may hold values from -6 to 6
- gauss_widths: int32 [2], replicated, may hold values from 2 to 4
- coeff_orders: int32 [21], replicated, may hold values from 0 to 2
- coefficients: float32 [32, 21, 6], P('visit'), may hold values from -4 to 4
- back_coeffs: float32 [32, 6], P('visit'), may hold values from -3 to 3
- masks: int32 [32, 512, 4096], P('visit', 'strip'), may hold values from 0 to 4095
- decor_kernel: float32 [32, 11, 11], P('visit'), may hold values from -0.6 to 0.6
Outputs:
- decorrelated: float32 [32, 512, 4096], P('visit', 'strip')
Inputs may be any that keep to these rules, and one draw needn't show every extreme that they name: `masks`: twelve mask planes a pixel.
All inputs are finite; a program needn't handle non-finite values.
Results may differ from a plain program's by a relative error of at most 0.0003.
Values sent between devices are 32-bit elements; how exact they have to be, the bound alone decides.
No kernel may reach another device: no remote copies, remote signals or barrier semaphores. Data moves between devices by JAX's collectives and lax.ppermute only.
A program may use at most 192 MiB of HBM per device.

v0:
```python
import jax
import jax.numpy as jnp
from jax import lax
from jax.sharding import PartitionSpec as P

KSIZE = 21
NBASIS = 21
NFILT = 8
NPOLY = 6
DKSIZE = 11
KHALF = 10
DHALF = 5


def extended(shard, sides, width):
    for axis, dim in sides:
        size, length = (lax.axis_size(axis), shard.shape[dim])
        up = [(i, (i + 1) % size) for i in range(size - 1)]
        down = [(j, i) for i, j in up]
        last = lax.slice_in_dim(shard, length - width, length, axis=dim)
        first = lax.slice_in_dim(shard, 0, width, axis=dim)
        before = lax.ppermute(last, axis, up)
        after = lax.ppermute(first, axis, down)
        shard = jnp.concatenate([before, shard, after], axis=dim)
    return shard


def kernel_table(gauss_widths):
    offsets = jnp.arange(KSIZE).astype(jnp.float32) - KHALF
    kernel_rows = []
    for family, degree in ((0, 4), (1, 2)):
        spread = 0.75 * gauss_widths[family].astype(jnp.float32)
        profile = jnp.exp(-offsets * offsets / (2.0 * spread * spread))
        profile = profile / jnp.sum(profile)
        scaled = offsets / spread
        for exponent in range(degree + 1):
            kernel_rows.append(scaled**exponent * profile)
    return jnp.stack(kernel_rows)


def basis_pairs():
    basis_list = []
    for family_base, degree in ((0, 4), (5, 2)):
        for exponent in range(degree + 1):
            for second in range(degree + 1 - exponent):
                basis_list.append((family_base + exponent, family_base + second))
    return basis_list


def band_matrix(kernels, out_len, half_width):
    in_len = out_len + 2 * half_width
    out_pos = jnp.arange(out_len)[:, None]
    in_pos = jnp.arange(in_len)[None, :]
    position = out_pos - in_pos + 2 * half_width
    onehot = (position[:, :, None] == jnp.arange(2 * half_width + 1)[None, None, :]).astype(
        jnp.float32
    )
    return jnp.einsum("oik,nk->noi", onehot, kernels, precision=lax.Precision.HIGHEST)


def monomials(row_pos, total_rows, col_total):
    ynorm = (2.0 * row_pos.astype(jnp.float32) + 1.0) / total_rows - 1.0
    xnorm = (2.0 * jnp.arange(col_total).astype(jnp.float32) + 1.0) / col_total - 1.0
    ygrid = jnp.broadcast_to(ynorm[:, None], (row_pos.shape[0], col_total))
    xgrid = jnp.broadcast_to(xnorm[None, :], (row_pos.shape[0], col_total))
    return jnp.stack(
        [jnp.ones_like(xgrid), xgrid, ygrid, xgrid * xgrid, xgrid * ygrid, ygrid * ygrid]
    )


def shards(
    science, template, gauss_widths, coeff_orders, coefficients, back_coeffs, masks, decor_kernel
):
    kernels = kernel_table(gauss_widths)
    row_count = template.shape[0]
    col_total = science.shape[2]
    visit_count = science.shape[0]
    vert_band = band_matrix(kernels, row_count, KHALF)
    rimmed = extended(template, (("strip", 0),), KHALF)
    own_filtered = jnp.einsum("nrs,sc->nrc", vert_band, rimmed, precision=lax.Precision.HIGHEST)
    vertical = lax.all_gather(own_filtered, "visit", axis=2, tiled=True)
    block_width = 128
    block_count = col_total // block_width
    padded_vert = jnp.pad(vertical, ((0, 0), (0, 0), (KHALF, block_width - KHALF)))
    main_part = padded_vert[:, :, :col_total].reshape(NFILT, row_count, block_count, block_width)
    next_part = padded_vert[:, :, block_width : col_total + block_width].reshape(
        NFILT, row_count, block_count, block_width
    )
    blocks = jnp.concatenate([main_part, next_part[:, :, :, : 2 * KHALF]], axis=3)
    col_band = band_matrix(kernels, block_width, KHALF)
    pair_list = basis_pairs()
    row_select = jnp.array([pair[0] for pair in pair_list], jnp.int32)
    col_select = jnp.array([pair[1] for pair in pair_list], jnp.int32)
    images = jnp.einsum(
        "krbs,kcs->krbc", blocks[row_select], col_band[col_select], precision=lax.Precision.HIGHEST
    )
    images = images.reshape(NBASIS, row_count, col_total)
    row_pos = lax.axis_index("strip") * row_count + jnp.arange(row_count)
    monomial_stack = monomials(row_pos, row_count * lax.axis_size("strip"), col_total)
    degrees = jnp.array([0, 1, 1, 2, 2, 2], jnp.int32)
    active = (degrees[None, :] <= coeff_orders[:, None]).astype(jnp.float32)
    effective = coefficients * active[None, :, :]
    model_image = jnp.zeros((visit_count, row_count, col_total), jnp.float32)
    for term in range(NPOLY):
        summed = jnp.einsum(
            "vk,krc->vrc", effective[:, :, term], images, precision=lax.Precision.HIGHEST
        )
        model_image = model_image + monomial_stack[term][None, :, :] * (
            summed + back_coeffs[:, term][:, None, None]
        )
    bad_pixel = jnp.bitwise_and(masks, 7) == 7
    differences = jnp.where(bad_pixel, jnp.zeros_like(model_image), science - model_image)
    rimmed_diff = extended(differences, (("strip", 1),), DHALF)
    tap_table = jnp.swapaxes(decor_kernel, 1, 2).reshape(visit_count * DKSIZE, DKSIZE)
    decor_band = band_matrix(tap_table, row_count, DHALF).reshape(
        visit_count, DKSIZE, row_count, row_count + 2 * DHALF
    )
    row_filtered = jnp.einsum(
        "vjrs,vsc->vjrc", decor_band, rimmed_diff, precision=lax.Precision.HIGHEST
    )
    padded_out = jnp.pad(row_filtered, ((0, 0), (0, 0), (0, 0), (DHALF, DHALF)))
    result = jnp.zeros((visit_count, row_count, col_total), jnp.float32)
    for col_tap in range(DKSIZE):
        first_col = 2 * DHALF - col_tap
        result = result + padded_out[:, col_tap, :, first_col : first_col + col_total]
    return result


def solution(mesh):
    return jax.shard_map(
        shards,
        mesh=mesh,
        in_specs=(
            P("visit", "strip", None),
            P("strip", "visit"),
            P(),
            P(),
            P("visit", None, None),
            P("visit", None),
            P("visit", "strip", None),
            P("visit", None, None),
        ),
        out_specs=P("visit", "strip", None),
        check_vma=False,
    )
```

profile of v0, /device:TPU:25, one launch (start us, length us, event | category | flops | bytes accessed | tf_op | source)
XLA Modules:
  0.0 436.7 jit_solution(7569935276805339708)
XLA Ops:
  6.5 0.0 all-gather.2.cloned.1.call-start
  6.5 0.7 fusion.107
  7.3 3.5 collective-permute-start
  10.8 4.2 collective-permute-start.1
  15.0 1.3 fusion.108
  17.6 0.6 exponential_reduce_fusion
  18.2 0.7 exponential_reduce_fusion.1
  18.9 1.2 multiply_multiply_fusion
  20.1 0.3 fusion.82
  20.5 0.0 copy-start.4
  20.5 0.0 copy-start.9
  20.5 0.0 collective-permute-done
  20.5 0.0 collective-permute-done.1
  20.5 2.2 fusion.84
  22.7 0.0 all-gather.2.cloned.1.call-update
  22.8 0.2 iota_compare_fusion
  23.0 0.6 fusion.78
  23.6 0.1 copy.36
  23.7 0.0 copy-done.4
  23.8 0.1 reshape.252
  23.8 0.0 copy-done.9
  23.9 0.0 copy-start.8
  23.9 0.0 copy-start.3
  23.9 0.0 copy-start.6
  23.9 0.0 copy-start.7
  23.9 0.0 copy-start.5
  23.9 0.7 gather_fusion.1
  24.6 0.0 copy-done.8
  24.6 0.0 copy-done.3
  24.6 0.3 slice_reduce_fusion
  24.9 0.0 copy-done.6
  24.9 0.0 copy-done.7
  24.9 0.1 compare_convert_fusion
  25.0 0.0 copy-done.5
  25.0 0.1 broadcast_multiply_fusion
  25.2 76.8 %all-gather.2.cloned.1.call-done = f32[8,64,4096]{2,1,0:T(8,128)} async-done(((f32[8,64,256]{2,1,0:T(8,128)}), f32[8,64,4096]{2,1,0:T(8,128)}) %all-gather.2.cloned.1.call-update) | async-done | bytes 8388624 | tf_op jit(solution)/shard_map/all_gather | solution.py:81
  102.0 10.2 %pad_slice_fusion.11 = (f32[8,64,4096]{2,1,0:T(8,128)S(1)}, f32[8,64,4096]{2,1,0:T(8,128)S(1)}) fusion(f32[8,64,4096]{2,1,0:T(8,128)} %all-gather.2.cloned.1.call-done), kind=kLoop, calls=%fused_computation.26 | loop fusion | bytes 25165824 | tf_op jit(solution)/shard_map/slice | solution.py:85
  112.2 5.0 %copy.49 = f32[64,8,32,128]{3,2,1,0:T(8,128)} copy(f32[64,8,32,128]{3,1,2,0:T(8,128)S(1)} %bitcast.48) | data formatting | bytes 16777216
  117.2 5.3 %copy.50 = f32[64,8,32,128]{3,2,1,0:T(8,128)} copy(f32[64,8,32,128]{3,1,2,0:T(8,128)S(1)} %bitcast.47) | data formatting | bytes 16777216
  122.6 0.0 slice-done
  122.6 0.0 slice-done.1
  122.6 9.9 %pad_maximum_fusion = f32[8,64,32,148]{3,2,1,0:T(8,128)} fusion(f32[8,64,32,20]{3,2,1,0:T(8,128)} %bitcast.52, f32[8,64,32,128]{3,2,1,0:T(8,128)S(1)} %bitcast.51), kind=kLoop, calls=%fused_computation.14 | loop fusion | flops 2424832 | bytes 19398656 | tf_op jit(solution)/shard_map/concatenate | solution.py:89
  132.5 21.9 %gather_fusion = f32[21,64,32,148]{3,2,1,0:T(8,128)} fusion(f32[8,64,32,148]{3,2,1,0:T(8,128)} %pad_maximum_fusion, s32[1024]{0:T(1024)S(1)} %pad_clamp_fusion.1), kind=kCustom, calls=%fused_computation | custom fusion | bytes 50921556 | tf_op jit(solution)/shard_map/gather | solution.py:95
  154.3 43.3 %fusion.80 = f32[21,64,32,128]{3,2,1,0:T(8,128)} fusion(f32[21,64,32,148]{3,2,1,0:T(8,128)} %gather_fusion, f32[21,128,148]{1,2,0:T(8,128)S(1)} %gather_fusion.1), kind=kOutput, calls=%fused_computation.62 | convolution fusion | flops 9776922624 | bytes 49072128 | tf_op jit(solution)/shard_map/krbs,kcs->krbc/dot_general | solution.py:94
  197.7 24.5 %reshape.229 = f32[21,64,4096]{2,1,0:T(8,128)} reshape(f32[21,64,32,128]{3,2,1,0:T(8,128)} %fusion.80) | data formatting | bytes 44040192 | tf_op jit(solution)/shard_map/reshape | solution.py:97
  222.1 33.1 %fusion.12 = f32[2,64,4096]{2,0,1:T(2,128)S(1)} fusion(f32[21,64,4096]{2,1,0:T(8,128)} %reshape.229, f32[2]{0:T(128)S(1)} %get-tuple-element.9, f32[2,21,6]{1,0,2:T(2,128)S(1)} %broadcast_multiply_fusion.1), kind=kOutput, calls=%fused_computation.27 | convolution fusion | flops 132644864 | bytes 24118784 | tf_op jit(solution)/shard_map/vk,krc->vrc/dot_general | solution.py:105
  255.3 0.0 copy-done
  255.3 27.0 %fusion.60 = f32[2,64,4096]{2,0,1:T(2,128)S(1)} fusion(f32[2,64,4096]{2,0,1:T(2,128)S(1)} %fusion.12, f32[21,64,4096]{2,1,0:T(8,128)S(1)} %copy-done, f32[2]{0:T(128)S(1)} %get-tuple-element.8, f32[4096]{0:T(1024)S(1)} %multiply_add_fusion, f32[2,21,6]{1,0,2:T(2,128)S(1)} %broadcast_multiply_fusion.1), kind=kOutput, calls=%fused_computation.43 | convolution fusion | flops 133693440 | bytes 26232320 | tf_op jit(solution)/shard_map/vk,krc->vrc/dot_general | solution.py:105
  282.2 26.3 %fusion.54 = f32[2,64,4096]{2,0,1:T(2,128)S(1)} fusion(f32[2,64,4096]{2,0,1:T(2,128)S(1)} %fusion.60, f32[21,64,4096]{2,1,0:T(8,128)S(1)} %copy-done, f32[2]{0:T(128)S(1)} %get-tuple-element.7, f32[64]{0:T(128)S(1)} %get-tuple-element.28, f32[2,21,6]{1,0,2:T(2,128)S(1)} %broadcast_multiply_fusion.1), kind=kOutput, calls=%fused_computation.41 | convolution fusion | flops 133693440 | bytes 26216448 | tf_op jit(solution)/shard_map/vk,krc->vrc/dot_general | solution.py:105
  308.5 26.8 %fusion.48 = f32[2,64,4096]{2,0,1:T(2,128)S(1)} fusion(f32[2,64,4096]{2,0,1:T(2,128)S(1)} %fusion.54, f32[21,64,4096]{2,1,0:T(8,128)S(1)} %copy-done, f32[2]{0:T(128)S(1)} %get-tuple-element.6, f32[4096]{0:T(1024)S(1)} %fusion.91, f32[2,21,6]{1,0,2:T(2,128)S(1)} %broadcast_multiply_fusion.1), kind=kOutput, calls=%fused_computation.39 | convolution fusion | flops 133693440 | bytes 26232320 | tf_op jit(solution)/shard_map/vk,krc->vrc/dot_general | solution.py:105
  335.3 0.0 copy-start.1
  335.3 0.0 copy-start.2
  335.3 26.9 %fusion.42 = f32[2,64,4096]{2,0,1:T(2,128)S(1)} fusion(f32[2,64,4096]{2,0,1:T(2,128)S(1)} %fusion.48, f32[21,64,4096]{2,1,0:T(8,128)S(1)} %copy-done, f32[2]{0:T(128)S(1)} %get-tuple-element.10, f32[64,4096]{1,0:T(8,128)S(1)} %broadcast_multiply_fusion, f32[2,21,6]{1,0,2:T(2,128)S(1)} %broadcast_multiply_fusion.1), kind=kOutput, calls=%fused_computation.37 | convolution fusion | flops 133693440 | bytes 27264512 | tf_op jit(solution)/shard_map/vk,krc->vrc/dot_general | solution.py:105
  362.2 0.0 copy-done.1
  362.3 29.8 %compare_select_fusion = f32[2,64,4096]{2,0,1:T(2,128)S(1)} fusion(f32[2,64,4096]{2,0,1:T(2,128)S(1)} %fusion.42, f32[21,64,4096]{2,1,0:T(8,128)S(1)} %copy-done, f32[2,64,4096]{2,1,0:T(8,128)S(1)} %copy-done.1, s32[2,64,4096]{2,1,0:T(8,128)S(1)} %copy-done.2, f32[2]{0:T(128)S(1)} %get-tuple-element.5, f32[64]{0:T(128)S(1)} %get-tuple-element.29, ...), kind=kOutput, calls=%fused_computation.44 | convolution fusion | flops 135790592 | bytes 30410752 | tf_op jit(solution)/shard_map/vk,krc->vrc/dot_general | solution.py:105
  392.1 3.2 collective-permute-start.2
  395.3 4.2 collective-permute-start.3
  399.5 0.5 convolution_bitcast_fusion
  400.0 0.1 copy.32
  400.2 1.5 collective-permute-done.2
  401.6 0.9 collective-permute-done.3
  402.5 1.3 maximum_bitcast_fusion
  403.8 19.0 %fusion.65 = f32[2,11,64,4096]{3,2,1,0:T(8,128)S(1)} fusion(f32[2,11,64,74]{3,2,1,0:T(8,128)S(1)} %bitcast.53, f32[2,74,4096,1]{2,0,1,3:T(2,128)S(1)} %maximum_bitcast_fusion), kind=kOutput, calls=%fused_computation.45 | convolution fusion | flops 5121245184 | bytes 25910272 | tf_op jit(solution)/shard_map/vjrs,vsc->vjrc/dot_general | solution.py:118
  422.8 6.8 %fusion.77 = f32[2,64,4096]{2,1,0:T(8,128)} fusion(f32[2,11,64,4096]{3,2,1,0:T(8,128)S(1)} %fusion.65), kind=kLoop, calls=%fused_computation.59 | loop fusion | flops 5242880 | bytes 27262976 | tf_op jit(solution)/shard_map/add | solution.py:125
  (18 shorter events, 0.2 us)
Async XLA Ops:
  6.5 95.5 %all-gather.2.cloned.1.call-start = ((), (), s32[]{:S(2)}) async-start(), calls=%async_computation | async-start | bytes 8912896 | tf_op jit(solution)/shard_map/all_gather | solution.py:81
  7.3 13.2 %collective-permute-start = (f32[10,256]{1,0:T(8,128)S(1)}, f32[10,256]{1,0:T(8,128)S(1)}, u32[]{:S(2)}, u32[]{:S(2)}) collective-permute-start(f32[10,256]{1,0:T(8,128)S(1)} %get-tuple-element.19), channel_id=1, source_target_pairs={{0,1},{1,2},{2,3},{3,4},{4,5},{5,6},{6,7},{8,9},{9,10},{10,11},{11... | collective-permute-start | bytes 30728 | tf_op jit(solution)/shard_map/ppermute | solution.py:22
  10.8 9.7 %collective-permute-start.1 = (f32[10,256]{1,0:T(8,128)S(1)}, f32[10,256]{1,0:T(8,128)S(1)}, u32[]{:S(2)}, u32[]{:S(2)}) collective-permute-start(f32[10,256]{1,0:T(8,128)S(1)} %get-tuple-element.20), channel_id=1, source_target_pairs={{1,0},{2,1},{3,2},{4,3},{5,4},{6,5},{7,6},{9,8},{10,9},{11,10},{12... | collective-permute-start | bytes 30728 | tf_op jit(solution)/shard_map/ppermute | solution.py:23
  20.5 3.3 copy-start.4
  20.5 3.3 copy-start.9
  23.9 0.7 copy-start.8
  23.9 0.8 copy-start.3
  23.9 1.1 copy-start.6
  23.9 1.1 copy-start.7
  23.9 1.1 copy-start.5
  117.2 5.4 %slice-start = ((s8[8388608]{0:T(1024)(128)(4,1)}), s8[4194304]{0:T(1024)(128)(4,1)S(1)}, s32[]{:S(2)}) async-start(s8[8388608]{0:T(1024)(128)(4,1)} %bitcast.49), calls=%async_computation.1 | async-start | bytes 8388608
  117.2 5.4 %slice-start.1 = ((s8[8388608]{0:T(1024)(128)(4,1)}), s8[4194304]{0:T(1024)(128)(4,1)S(1)}, s32[]{:S(2)}) async-start(s8[8388608]{0:T(1024)(128)(4,1)} %bitcast.49), calls=%async_computation.2 | async-start | bytes 8388608
  222.1 33.1 %copy-start = (f32[21,64,4096]{2,1,0:T(8,128)S(1)}, f32[21,64,4096]{2,1,0:T(8,128)}, u32[]{:S(2)}) copy-start(f32[21,64,4096]{2,1,0:T(8,128)} %reshape.229) | copy-start | bytes 66060292
  335.3 27.0 %copy-start.1 = (f32[2,64,4096]{2,1,0:T(8,128)S(1)}, f32[2,64,4096]{2,1,0:T(8,128)}, u32[]{:S(2)}) copy-start(f32[2,64,4096]{2,1,0:T(8,128)} %param.11) | copy-start | bytes 6291460
  335.3 27.0 %copy-start.2 = (s32[2,64,4096]{2,1,0:T(8,128)S(1)}, s32[2,64,4096]{2,1,0:T(8,128)}, u32[]{:S(2)}) copy-start(s32[2,64,4096]{2,1,0:T(8,128)} %param.17) | copy-start | bytes 6291460
  392.1 9.6 %collective-permute-start.2 = (f32[2,5,4096]{2,0,1:T(2,128)S(1)}, f32[2,5,4096]{2,0,1:T(2,128)S(1)}, u32[]{:S(2)}, u32[]{:S(2)}) collective-permute-start(f32[2,5,4096]{2,0,1:T(2,128)S(1)} %get-tuple-element.17), channel_id=1, source_target_pairs={{0,1},{1,2},{2,3},{3,4},{4,5},{5,6},{6,7},{8,9},{9,10},{10,11},{11... | collective-permute-start | bytes 491528 | tf_op jit(solution)/shard_map/ppermute | solution.py:22
  395.3 7.2 %collective-permute-start.3 = (f32[2,5,4096]{2,0,1:T(2,128)S(1)}, f32[2,5,4096]{2,0,1:T(2,128)S(1)}, u32[]{:S(2)}, u32[]{:S(2)}) collective-permute-start(f32[2,5,4096]{2,0,1:T(2,128)S(1)} %get-tuple-element.18), channel_id=1, source_target_pairs={{1,0},{2,1},{3,2},{4,3},{5,4},{6,5},{7,6},{9,8},{10,9},{11,10},{12... | collective-permute-start | bytes 491528 | tf_op jit(solution)/shard_map/ppermute | solution.py:23
Sparse Core Ops, SparseCore 0:
  22.9 79.0 all-gather.1
where the time goes:
time: 443 us; the launch traced here: 437 us
  matrix products  236 us (53%)
  waiting for transfers between devices  79.2 us (18%)
  local copies, waits for them, and re-layouts  70.3 us (16%)
  other arithmetic  21 us (5%)
  between operations  15.2 us (3%)
  starting transfers between devices  15.1 us (3%)
    dot_general x6, matrix products, shards(): jnp.einsum('vk,krc->vrc', effective[:, :, term], images, precision=lax.Pr...  170 us
    all_gather x1, waiting for transfers between devices, shards(): vertical = lax.all_gather(own_filtered, 'visit', axis=2, tiled=True)  76.8 us
    dot_general x1, matrix products, shards(): jnp.einsum('krbs,kcs->krbc', blocks[row_select], col_band[col_select], pr...  43.3 us
    reshape x1, local copies, waits for them, and re-layouts, shards(): images = images.reshape(NBASIS, row_count, col_total)  24.5 us
    gather x1, local copies, waits for them, and re-layouts, shards(): blocks[row_select]  21.9 us
    dot_general x1, matrix products, shards(): jnp.einsum('vjrs,vsc->vjrc', decor_band, rimmed_diff, precision=lax.Preci...  19 us
    unnamed x26, local copies, waits for them, and re-layouts  10.4 us
    slice x1, local copies, waits for them, and re-layouts, shards(): padded_vert[:, :, :col_total]  10.2 us
  transfers between devices with their start and end apart: 5, of which 3 were waited for; matrix products, arithmetic and copies ran while one was open for 2% of the time, Pallas kernels for 0%

commit v1 on v0

v1 whole, which is shorter than its diff:
```python
import jax
import jax.numpy as jnp
from jax import lax
from jax.experimental import pallas as pl
from jax.experimental.pallas import tpu as pltpu
from jax.sharding import PartitionSpec as P

KSIZE = 21
NBASIS = 21
NFILT = 8
NPOLY = 6
DKSIZE = 11
KHALF = 10
DHALF = 5
LANES = 128
CHUNK = 512
TROWS = 96
HALFROWS = 40
MROWS = 6 * HALFROWS
KWIN = 64
DROWS = 80
F32 = jnp.float32
BF16 = jnp.bfloat16


def basis_pairs():
    basis_list = []
    for family_base, degree in ((0, 4), (5, 2)):
        for exponent in range(degree + 1):
            for second in range(degree + 1 - exponent):
                basis_list.append((family_base + exponent, family_base + second))
    return basis_list


def kernel_table(gauss_widths):
    offsets = jnp.arange(KSIZE).astype(F32) - KHALF
    kernel_rows = []
    for family, degree in ((0, 4), (1, 2)):
        spread = 0.75 * gauss_widths[family].astype(F32)
        profile = jnp.exp(-offsets * offsets / (2.0 * spread * spread))
        profile = profile / jnp.sum(profile)
        scaled = offsets / spread
        for exponent in range(degree + 1):
            kernel_rows.append(scaled**exponent * profile)
    return jnp.stack(kernel_rows)


def high_part(x):
    return lax.reduce_precision(x, 8, 7)


def split(x):
    high = x.astype(BF16)
    return high, (x - high.astype(F32)).astype(BF16)


def strip_rows_norm(meta, half, strip_rows):
    rows = lax.broadcasted_iota(jnp.int32, (HALFROWS, LANES), 0) + (
        meta[0] * strip_rows - 8 + half * HALFROWS
    )
    return (2.0 * rows.astype(F32) + 1.0) / meta[2].astype(F32) - 1.0


def prepare(strip_rows, meta, filters, taps, decor_base, col_weights, row_weights, decor_weights):
    visits = decor_weights.shape[0]
    source = lax.broadcasted_iota(jnp.int32, (LANES, LANES), 0)
    target = lax.broadcasted_iota(jnp.int32, (LANES, LANES), 1)
    near = jnp.abs(target - source) <= KHALF
    for j in range(NFILT):
        lanes = slice(j * LANES, (j + 1) * LANES)
        flat = jnp.broadcast_to(filters[j][None, :], (LANES, LANES))
        ring = pltpu.roll(flat, 0, 1, stride=1, stride_axis=0)
        high = ring.astype(BF16).astype(F32)
        low = ring - high
        col_weights[:LANES, lanes] = jnp.where(near, high, 0.0).astype(BF16)
        col_weights[LANES : 2 * LANES, lanes] = jnp.where(near, high, 0.0).astype(BF16)
        col_weights[2 * LANES : 3 * LANES, lanes] = jnp.where(near, low, 0.0).astype(BF16)
        side_high = jnp.where(near, 0.0, high)
        side_low = jnp.where(near, 0.0, low)
        packed = side_high + pltpu.roll(side_high, 20, 0) + pltpu.roll(side_low, 40, 0)
        col_weights[3 * LANES :, lanes] = packed.astype(BF16)
    for half in range(2):
        yn = strip_rows_norm(meta, half, strip_rows)
        for tile in range(4):
            lanes = slice(tile * LANES, (tile + 1) * LANES)
            parts = []
            for s in range(visits):
                rolled = []
                for t in range(NPOLY):
                    flat = jnp.broadcast_to(taps[s * NPOLY + t, lanes][None, :], (HALFROWS, LANES))
                    rolled.append(pltpu.roll(flat, 8 * half, 1, stride=1, stride_axis=0))
                parts.append(rolled[0] + yn * (rolled[2] + yn * rolled[5]))
                parts.append(rolled[1] + yn * rolled[4])
                parts.append(rolled[3])
            high, low = split(jnp.concatenate(parts, axis=0))
            row_weights[half, :MROWS, lanes] = high
            row_weights[half, MROWS:, lanes] = low
    for s in range(visits):
        for b in range(DKSIZE):
            flat = jnp.broadcast_to(decor_base[s * DKSIZE + b][None, :], (strip_rows, 2 * LANES))
            turned = pltpu.roll(flat, 3, 1, stride=1, stride_axis=0)
            decor_weights[s, b * strip_rows : (b + 1) * strip_rows, :] = turned.astype(BF16)


def body(
    meta,
    back,
    own,
    other,
    col_weights,
    row_weights,
    decor_weights,
    science,
    masks,
    halo_up,
    halo_down,
    out,
    high_filtered,
    low_filtered,
    carry,
):
    step = pl.program_id(0)
    steps = pl.num_programs(0)
    core = meta[1]
    visits = science.shape[0]
    strip_rows = science.shape[1]

    @pl.when(step == 0)
    def clear():
        carry[...] = jnp.zeros_like(carry)

    mine, theirs = own[step], other[step]
    even = jnp.where(core == 0, mine, theirs)
    odd = jnp.where(core == 0, theirs, mine)
    before = jnp.maximum(step - 1, 0)
    after = jnp.minimum(step + 1, steps - 1)
    left = jnp.where(core == 0, other[before, :, LANES:], own[before, :, LANES:])
    left = jnp.where(step > 0, left, 0.0)
    right = jnp.where(core == 0, own[after, :, :LANES], other[after, :, :LANES])
    right = jnp.where(step < steps - 1, right, 0.0)
    blocks = [left, even[:, :LANES], even[:, LANES:], odd[:, :LANES], odd[:, LANES:], right]
    lane = lax.broadcasted_iota(jnp.int32, (TROWS, LANES), 1)
    stacked = []
    for b in range(4):
        high, low = split(blocks[b + 1])
        side = jnp.where(lane < KHALF, blocks[b + 2], jnp.where(lane >= LANES - KHALF, blocks[b], 0.0))
        side_high = side.astype(BF16).astype(F32)
        side_low = side - side_high
        packed = side_high + pltpu.roll(side_low, 20, 1) + pltpu.roll(side_high, 40, 1)
        stacked.append(jnp.concatenate([high, low, high, packed.astype(BF16)], axis=1))
    lhs = jnp.concatenate(stacked, axis=0)
    for pair in range(4):
        filtered = jnp.dot(
            lhs, col_weights[:, 256 * pair : 256 * (pair + 1)], preferred_element_type=F32
        )
        for inner in range(2):
            first = (2 * pair + inner) * TROWS
            for b in range(4):
                high, low = split(
                    filtered[TROWS * b : TROWS * (b + 1), LANES * inner : LANES * (inner + 1)]
                )
                high_filtered[first : first + TROWS, LANES * b : LANES * (b + 1)] = high
                low_filtered[first : first + TROWS, LANES * b : LANES * (b + 1)] = low

    columns = lax.broadcasted_iota(jnp.int32, (HALFROWS, CHUNK), 1) + step * CHUNK
    xn = (2.0 * columns.astype(F32) + 1.0) / float(steps * CHUNK) - 1.0
    models = [[None, None] for _ in range(visits)]
    for half in range(2):
        starts = [j * TROWS + 32 * half for j in range(NFILT)]
        rhs_high = jnp.concatenate([high_filtered[r : r + KWIN, :] for r in starts], axis=0)
        rhs_low = jnp.concatenate([low_filtered[r : r + KWIN, :] for r in starts], axis=0)
        wide = jnp.dot(row_weights[half], rhs_high, preferred_element_type=F32)
        rest = jnp.dot(row_weights[half, :MROWS, :], rhs_low, preferred_element_type=F32)
        summed = wide[:MROWS] + wide[MROWS:] + rest
        yn = strip_rows_norm(meta, half, strip_rows)[:, :1]
        for s in range(visits):
            base = s * 3 * HALFROWS
            back0 = back[s, 0] + yn * (back[s, 2] + yn * back[s, 5])
            back1 = back[s, 1] + yn * back[s, 4]
            g0 = summed[base : base + HALFROWS] + back0
            g1 = summed[base + HALFROWS : base + 2 * HALFROWS] + back1
            g2 = summed[base + 2 * HALFROWS : base + 3 * HALFROWS] + back[s, 3]
            models[s][half] = g0 + xn * (g1 + xn * g2)

    edge_lane = lax.broadcasted_iota(jnp.int32, (strip_rows, LANES), 1)
    start = pl.multiple_of(step * CHUNK, CHUNK)
    for s in range(visits):
        model = jnp.concatenate(models[s], axis=0)
        data = jnp.concatenate([halo_up[s, :8], science[s], halo_down[s, :8]], axis=0)
        fine = jnp.where(jnp.bitwise_and(masks[s], 7) == 7, 0.0, 1.0)
        good = jnp.concatenate([halo_up[s, 8:], fine, halo_down[s, 8:]], axis=0)
        diff = jnp.where(good > 0.5, data - model, 0.0)
        high, low = split(diff)
        rhs = jnp.concatenate([high, low, high, jnp.zeros((16, CHUNK), BF16)], axis=0)
        product = jnp.dot(decor_weights[s], rhs, preferred_element_type=F32)
        total = product[DHALF * strip_rows : (DHALF + 1) * strip_rows]
        to_right = jnp.zeros((strip_rows, LANES), F32)
        to_left = jnp.zeros((strip_rows, LANES), F32)
        for b in range(DKSIZE):
            shift = b - DHALF
            if shift == 0:
                continue
            turned = pltpu.roll(
                product[b * strip_rows : (b + 1) * strip_rows], shift % CHUNK, 1
            )
            if shift > 0:
                first = turned[:, :LANES]
                to_right = to_right + jnp.where(edge_lane < shift, first, 0.0)
                first = jnp.where(edge_lane < shift, 0.0, first)
                turned = jnp.concatenate([first, turned[:, LANES:]], axis=1)
            else:
                last = turned[:, CHUNK - LANES :]
                to_left = to_left + jnp.where(edge_lane >= LANES + shift, last, 0.0)
                last = jnp.where(edge_lane >= LANES + shift, 0.0, last)
                turned = jnp.concatenate([turned[:, : CHUNK - LANES], last], axis=1)
            total = total + turned
        out[s, :, pl.ds(start, LANES)] = total[:, :LANES] + carry[s]
        out[s, :, pl.ds(start + LANES, CHUNK - LANES)] = total[:, LANES:]
        carry[s] = to_right

        @pl.when(step > 0)
        def add_left():
            before_start = pl.multiple_of(start - LANES, LANES)
            out[s, :, pl.ds(before_start, LANES)] += to_left


def build_weights(visits, strip_rows, meta, filters, taps, decor_base):
    return pl.pallas_call(
        lambda *refs: prepare(strip_rows, *refs),
        out_shape=[
            jax.ShapeDtypeStruct((4 * LANES, NFILT * LANES), BF16),
            jax.ShapeDtypeStruct((2, 2 * MROWS, NFILT * KWIN), BF16),
            jax.ShapeDtypeStruct((visits, DKSIZE * strip_rows, 2 * LANES), BF16),
        ],
        in_specs=[pl.BlockSpec(memory_space=pltpu.SMEM)]
        + [pl.BlockSpec(memory_space=pltpu.VMEM)] * 3,
        compiler_params=pltpu.CompilerParams(vmem_limit_bytes=24 * 1024 * 1024),
        cost_estimate=pl.CostEstimate(flops=10**8, bytes_accessed=4 * 2**20, transcendentals=0),
    )(meta, filters, taps, decor_base)


def whole(array):
    return pl.BlockSpec(array.shape, lambda i: (0,) * len(array.shape))


def fused(
    meta,
    back,
    own,
    other,
    col_weights,
    row_weights,
    decor_weights,
    science,
    masks,
    halo_up,
    halo_down,
):
    visits, strip_rows, col_total = science.shape
    out = jax.ShapeDtypeStruct(science.shape, F32)
    return pl.pallas_call(
        body,
        grid=(col_total // CHUNK,),
        out_shape=out,
        in_specs=[
            pl.BlockSpec(memory_space=pltpu.SMEM),
            pl.BlockSpec(memory_space=pltpu.SMEM),
            whole(own),
            whole(other),
            whole(col_weights),
            whole(row_weights),
            whole(decor_weights),
            pl.BlockSpec((visits, strip_rows, CHUNK), lambda i: (0, 0, i)),
            pl.BlockSpec((visits, strip_rows, CHUNK), lambda i: (0, 0, i)),
            pl.BlockSpec((visits, 16, CHUNK), lambda i: (0, 0, i)),
            pl.BlockSpec((visits, 16, CHUNK), lambda i: (0, 0, i)),
        ],
        out_specs=whole(out),
        scratch_shapes=[
            pltpu.VMEM((NFILT * TROWS, CHUNK), BF16),
            pltpu.VMEM((NFILT * TROWS, CHUNK), BF16),
            pltpu.VMEM((visits, strip_rows, LANES), F32),
        ],
        compiler_params=pltpu.CompilerParams(
            dimension_semantics=("arbitrary",), vmem_limit_bytes=48 * 1024 * 1024
        ),
        cost_estimate=pl.CostEstimate(
            flops=14 * 10**9, bytes_accessed=10 * 2**20, transcendentals=0
        ),
    )(
        meta,
        back,
        own,
        other,
        col_weights,
        row_weights,
        decor_weights,
        science,
        masks,
        halo_up,
        halo_down,
    )


def shards(
    science, template, gauss_widths, coeff_orders, coefficients, back_coeffs, masks, decor_kernel
):
    visits, strip_rows, col_total = science.shape
    strips = lax.axis_size("strip")
    strip = lax.axis_index("strip")
    core = lax.axis_index("visit") % 2
    up = [(i, i + 1) for i in range(strips - 1)]
    down = [(i + 1, i) for i in range(strips - 1)]

    above = lax.ppermute(template[strip_rows - 16 :], "strip", up)
    below = lax.ppermute(template[:16], "strip", down)

    rimmed = jnp.concatenate([above, template, below], axis=0)
    rimmed, science_late, masks_late, gauss_widths, coefficients, decor_kernel = lax.optimization_barrier(
        (rimmed, science, masks, gauss_widths, coefficients, decor_kernel)
    )

    def edge(rows):
        good = jnp.where(jnp.bitwise_and(masks_late[:, rows], 7) == 7, 0.0, 1.0)
        return jnp.concatenate([science_late[:, rows], good], axis=1)

    halo_up = lax.ppermute(edge(slice(strip_rows - 8, strip_rows)), "strip", up)
    halo_down = lax.ppermute(edge(slice(0, 8)), "strip", down)

    kernels = kernel_table(gauss_widths)
    filters = jnp.roll(jnp.pad(kernels, ((0, 0), (0, LANES - KSIZE))), -KHALF, axis=1)
    degrees = jnp.array([0, 1, 1, 2, 2, 2], jnp.int32)
    active = (degrees[None, :] <= coeff_orders[:, None]).astype(F32)
    effective = coefficients * active[None, :, :]
    pairs = basis_pairs()
    row_onehot = jax.nn.one_hot(jnp.array([p[0] for p in pairs]), NFILT, dtype=F32)
    col_onehot = jax.nn.one_hot(jnp.array([p[1] for p in pairs]), NFILT, dtype=F32)
    by_row = jnp.einsum(
        "ki,id->kd", row_onehot, kernels, precision=lax.Precision.HIGHEST
    )
    placed = col_onehot[:, :, None] * by_row[:, None, ::-1]
    taps = jnp.einsum("skt,kjd->stjd", effective, placed, precision=lax.Precision.HIGHEST)
    taps = jnp.pad(taps, ((0, 0), (0, 0), (0, 0), (0, KWIN - KSIZE)))
    taps = taps.reshape(visits * NPOLY, NFILT * KWIN // LANES, LANES)
    taps = jnp.roll(taps, -2, axis=2).reshape(visits * NPOLY, NFILT * KWIN)

    flipped = jnp.swapaxes(decor_kernel[:, ::-1, :], 1, 2)
    decor_high = high_part(flipped)
    wide = ((0, 0), (0, 0), (0, DROWS - DKSIZE))
    decor_base = jnp.concatenate(
        [
            jnp.pad(decor_high, wide),
            jnp.pad(decor_high, wide),
            jnp.pad(flipped - decor_high, wide),
            jnp.zeros((visits, DKSIZE, 16), F32),
        ],
        axis=2,
    ).reshape(visits * DKSIZE, 2 * LANES)

    size = lax.axis_size("visit")
    groups = [[i for i in range(size) if i % 2 == c] for c in range(2)]
    chips = size // 2
    own = lax.all_to_all(
        jnp.broadcast_to(rimmed[None], (chips,) + rimmed.shape),
        "visit",
        0,
        0,
        axis_index_groups=groups,
    )
    other = lax.ppermute(own, "visit", [(i, i ^ 1) for i in range(size)])

    meta = jnp.stack([strip, core, strip_rows * strips]).astype(jnp.int32)
    weights = build_weights(visits, strip_rows, meta, filters, taps, decor_base)
    return fused(
        meta, back_coeffs, own, other, *weights, science, masks, halo_up, halo_down
    )


def solution(mesh):
    return jax.shard_map(
        shards,
        mesh=mesh,
        in_specs=(
            P("visit", "strip", None),
            P("strip", "visit"),
            P(),
            P(),
            P("visit", None, None),
            P("visit", None),
            P("visit", "strip", None),
            P("visit", None, None),
        ),
        out_specs=P("visit", "strip", None),
        check_vma=False,
    )
```

time: 443 us -> 74 us (0.17); the launches traced: 437 us -> 72.9 us
  matrix products: 236 us -> 0.46 us
  waiting for transfers between devices: 79.2 us -> 11.1 us
  local copies, waits for them, and re-layouts: 70.3 us -> 4.38 us
  Pallas kernels: 0 us -> 25.4 us
  other arithmetic: 21 us -> 7.25 us
  between operations: 15.2 us -> 1.47 us
  starting transfers between devices: 15.1 us -> 22.8 us
    dot_general x12 -> x2, matrix products: 236 us -> 0.46 us  [the longest x1 0.27 us: shards(): jnp.einsum('skt,kjd->stjd', effective, placed, precision=lax.Precision.HI...]
    all_gather x1 -> x0, waiting for transfers between devices: 76.8 us -> none  [shards(): vertical = lax.all_gather(own_filtered, 'visit', axis=2, tiled=True)]
    pallas_call x0 -> x2, Pallas kernels: none -> 25.4 us  [the longest x1 23.9 us: fused(): pl.pallas_call(body, grid=(col_total // CHUNK,), out_shape=out, in_specs=...]
    reshape x2, local copies, waits for them, and re-layouts: 24.6 us -> 0.09 us  [the longest x1 0.08 us: shards(): taps = taps.reshape(visits * NPOLY, NFILT * KWIN // LANES, LANES)]
    gather x2 -> x0, local copies, waits for them, and re-layouts: 22.5 us -> none  [the longest x1 21.9 us: shards(): blocks[row_select]]
    unnamed x26 -> x9, local copies, waits for them, and re-layouts: 10.4 us -> 0.04 us
    slice x5 -> x4, local copies, waits for them, and re-layouts: 12.5 us -> 2.2 us  [the longest x1 1.31 us: kernel_table(): spread = 0.75 * gauss_widths[family].astype(F32)]
    concatenate x2 -> x6, other arithmetic: 11.2 us -> 1.98 us  [the longest x2 0.86 us: edge(): return jnp.concatenate([science_late[:, rows], good], axis=1)]
  transfers between devices with their start and end apart: 5 -> 6, of which waited for: 3 -> 2; matrix products, arithmetic and copies ran while one was open for 2% -> 7% of each run, Pallas kernels for 0% -> 2%
where the time goes in v1:
time: 74 us; the launch traced here: 72.9 us
  Pallas kernels  25.4 us (34%)
  starting transfers between devices  22.8 us (31%)
  waiting for transfers between devices  11.1 us (15%)
  other arithmetic  7.25 us (10%)
  local copies, waits for them, and re-layouts  4.38 us (6%)
  between operations  1.47 us (2%)
    pallas_call x1, Pallas kernels, fused(): pl.pallas_call(body, grid=(col_total // CHUNK,), out_shape=out, in_specs=...  23.9 us
    ppermute x1, waiting for transfers between devices, shards(): halo_up = lax.ppermute(edge(slice(strip_rows - 8, strip_rows)), 'strip', up)  9.31 us
    all_to_all x1, starting transfers between devices, shards(): lax.all_to_all(jnp.broadcast_to(rimmed[None], (chips,) + rimmed.shape), '...  6.83 us
    ppermute x1, starting transfers between devices, shards(): halo_down = lax.ppermute(edge(slice(0, 8)), 'strip', down)  5.16 us
    ppermute x1, starting transfers between devices, shards(): below = lax.ppermute(template[:16], 'strip', down)  4.22 us
    ppermute x1, starting transfers between devices, shards(): above = lax.ppermute(template[strip_rows - 16:], 'strip', up)  3.53 us
    ppermute x1, starting transfers between devices, shards(): halo_up = lax.ppermute(edge(slice(strip_rows - 8, strip_rows)), 'strip', up)  2.22 us
    all_to_all x1, waiting for transfers between devices, shards(): lax.all_to_all(jnp.broadcast_to(rimmed[None], (chips,) + rimmed.shape), '...  1.79 us
  transfers between devices with their start and end apart: 6, of which 2 were waited for; matrix products, arithmetic and copies ran while one was open for 7% of the time, Pallas kernels for 2%

profile of v1, /device:TPU:25, one launch (start us, length us, event | category | flops | bytes accessed | tf_op | source)
XLA Modules:
  0.0 72.9 jit_solution(12232100501256131879)
XLA Ops:
  0.0 0.7 %fusion.18 = (f32[16,256]{1,0:T(8,128)S(1)}, f32[16,256]{1,0:T(8,128)S(1)}) fusion(f32[64,256]{1,0:T(8,128)} %param.12), kind=kLoop, calls=%fused_computation.45 | loop fusion | bytes 65536 | tf_op jit(solution)/shard_map/slice | solution.py:315
  0.7 3.5 %collective-permute-start = (f32[16,256]{1,0:T(8,128)S(1)}, f32[16,256]{1,0:T(8,128)S(1)}, u32[]{:S(2)}, u32[]{:S(2)}) collective-permute-start(f32[16,256]{1,0:T(8,128)S(1)} %get-tuple-element.31), channel_id=1, source_target_pairs={{0,1},{1,2},{2,3},{3,4},{4,5},{5,6},{6,7},{8,9},{9,10},{10,11},{11... | collective-permute-start | bytes 49160 | tf_op jit(solution)/shard_map/ppermute | solution.py:315
  4.3 4.2 %collective-permute-start.1 = (f32[16,256]{1,0:T(8,128)S(1)}, f32[16,256]{1,0:T(8,128)S(1)}, u32[]{:S(2)}, u32[]{:S(2)}) collective-permute-start(f32[16,256]{1,0:T(8,128)S(1)} %get-tuple-element.32), channel_id=1, source_target_pairs={{1,0},{2,1},{3,2},{4,3},{5,4},{6,5},{7,6},{9,8},{10,9},{11,10},{12... | collective-permute-start | bytes 49160 | tf_op jit(solution)/shard_map/ppermute | solution.py:316
  8.5 0.7 fusion.12
  9.2 0.7 %compare_convert_fusion = f32[21,6]{0,1:T(8,128)S(1)} fusion(s32[21]{0:T(128)} %param.14, s32[6]{0:T(128)} %constant.54.clone), kind=kLoop, calls=%fused_computation.27 | loop fusion | flops 252 | bytes 612 | tf_op jit(solution)/shard_map/convert_element_type | solution.py:333
  9.9 0.1 pad_add_fusion.refs_0_.meta
  10.0 0.1 pad.27.clone
  10.1 0.0 collective-permute-done
  10.1 0.0 collective-permute-done.1
  10.1 0.8 %pad_maximum_fusion.2 = f32[96,256]{1,0:T(8,128)S(1)} fusion(f32[16,256]{1,0:T(8,128)S(1)} %collective-permute-done.1, f32[64,256]{1,0:T(8,128)} %param.12, f32[16,256]{1,0:T(8,128)S(1)} %collective-permute-done), kind=kLoop, calls=%fused_computation.6 | loop fusion | flops 49152 | bytes 196608 | tf_op jit(solution)/shard_map/concatenate | solution.py:318
  10.9 1.3 %fusion.19 = (s32[1]{0:T(128)}, s32[1]{0:T(128)}) fusion(s32[2]{0:T(128)} %param.13), kind=kLoop, calls=%fused_computation.46 | loop fusion | bytes 16 | tf_op jit(solution)/shard_map/slice | solution.py:39
  13.5 0.7 exponential_reduce_fusion.1
  14.2 0.6 exponential_reduce_fusion
  14.8 1.2 %multiply_multiply_fusion = (f32[1,21]{1,0:T(1,128)S(1)}, f32[1,21]{1,0:T(1,128)S(1)}, f32[1,21]{1,0:T(1,128)S(1)}, f32[1,21]{1,0:T(1,128)S(1)}) fusion(f32[]{:T(128)} %bitcast.5, f32[]{:T(128)} %exponential_reduce_fusion, f32[]{:T(128)} %bitcast.4, f32[]{:T(128)} %exponential_reduce_fusion.1, f32[]{:T(128)} %bitcast.2, f32[]{:T(128)} %bitcast.3), kind=kLoop, calls=%fused_computation.31 | loop fusion | flops 315 | bytes 360 | tf_op jit(solution)/shard_map/mul | solution.py:44
  16.0 0.8 %copy.19 = f32[2,11,11]{1,0,2:T(2,128)S(1)} copy(f32[2,11,11]{2,0,1:T(2,128)} %param.18) | data formatting | bytes 1936 | tf_op jit(solution)/shard_map/optimization_barrier | solution.py:319
  16.8 0.1 rev.7
  17.0 0.9 %broadcast_in_dim.27 = f32[8,96,256]{2,1,0:T(8,128)} broadcast(f32[96,256]{1,0:T(8,128)S(1)} %pad_maximum_fusion.2), dimensions={1,2} | broadcast | bytes 884736 | tf_op jit(solution)/shard_map/broadcast_in_dim | solution.py:364
  17.9 0.0 copy-start.2
  17.9 6.8 %all-to-all-start = ((f32[8,96,256]{2,1,0:T(8,128)}), f32[8,96,256]{2,1,0:T(8,128)S(1)}, u32[]{:S(2)}, u32[]{:S(2)}) async-start(f32[8,96,256]{2,1,0:T(8,128)} %broadcast_in_dim.27), calls=%async_computation | async-start | bytes 1572864 | tf_op jit(solution)/shard_map/all_to_all | solution.py:363
  24.8 0.0 copy-start.1
  24.8 1.3 %fusion.1 = (f32[2,8,4096]{2,1,0:T(8,128)S(1)}, f32[2,8,4096]{2,1,0:T(8,128)S(1)}, f32[2,8,4096]{2,1,0:T(8,128)S(1)}, f32[2,8,4096]{2,1,0:T(8,128)S(1)}) fusion(s32[2,64,4096]{2,1,0:T(8,128)} %masks.1, f32[2,64,4096]{2,1,0:T(8,128)} %science.1), kind=kLoop, calls=%fused_computation.5 | loop fusion | flops 393216 | bytes 2097152 | tf_op jit(solution)/shard_map/jit(_where)/select_n | solution.py:324
  26.0 0.0 copy-start
  26.1 0.1 fusion.8
  26.3 0.0 copy-done.2
  26.3 0.2 fusion.9
  26.5 0.1 rev.6
  26.6 2.2 %collective-permute-start.3 = (f32[2,16,4096]{2,1,0:T(8,128)S(1)}, f32[2,16,4096]{2,1,0:T(8,128)S(1)}, u32[]{:S(2)}, u32[]{:S(2)}) collective-permute-start(f32[2,16,4096]{2,1,0:T(8,128)S(1)} %pad_maximum_fusion), channel_id=1, source_target_pairs={{0,1},{1,2},{2,3},{3,4},{4,5},{5,6},{6,7},{8,9},{9,10},{10,11},{11... | collective-permute-start | bytes 1572872 | tf_op jit(solution)/shard_map/ppermute | solution.py:327
  28.8 0.8 %pad_maximum_fusion.1 = f32[2,16,4096]{2,1,0:T(8,128)} fusion(f32[2,8,4096]{2,1,0:T(8,128)S(1)} %get-tuple-element.29, f32[2,8,4096]{2,1,0:T(8,128)S(1)} %get-tuple-element.41), kind=kLoop, calls=%fused_computation.1 | loop fusion | flops 131072 | bytes 1048576 | tf_op jit(solution)/shard_map/concatenate | solution.py:325
  29.6 5.2 %collective-permute-start.4 = (f32[2,16,4096]{2,1,0:T(8,128)}, f32[2,16,4096]{2,1,0:T(8,128)S(1)}, u32[]{:S(2)}, u32[]{:S(2)}) collective-permute-start(f32[2,16,4096]{2,1,0:T(8,128)} %pad_maximum_fusion.1), channel_id=1, source_target_pairs={{1,0},{2,1},{3,2},{4,3},{5,4},{6,5},{7,6},{9,8},{10,9},{11,10},{12... | collective-permute-start | bytes 1572872 | tf_op jit(solution)/shard_map/ppermute | solution.py:328
  34.8 1.8 %all-to-all-done.own = f32[8,96,256]{2,1,0:T(8,128)S(1)} async-done(((f32[8,96,256]{2,1,0:T(8,128)}), f32[8,96,256]{2,1,0:T(8,128)S(1)}, u32[]{:S(2)}, u32[]{:S(2)}) %all-to-all-start) | async-done | bytes 786464 | tf_op jit(solution)/shard_map/all_to_all | solution.py:363
  36.6 0.9 %collective-permute-start.2 = (f32[8,96,256]{2,1,0:T(8,128)S(1)}, f32[8,96,256]{2,1,0:T(8,128)S(1)}, u32[]{:S(2)}, u32[]{:S(2)}) collective-permute-start(f32[8,96,256]{2,1,0:T(8,128)S(1)} %all-to-all-done.own), channel_id=1, source_target_pairs={{0,8},{8,0},{16,24},{24,16},{32,40},{40,32},{48,56},{56,48},{64,72... | collective-permute-start | bytes 2359304 | tf_op jit(solution)/shard_map/ppermute | solution.py:370
  37.4 0.0 copy-done.1
  37.4 0.3 fusion.2
  37.7 0.1 reshape.151
  37.8 0.1 slice.53
  37.9 0.1 pad_maximum_fusion.3
  38.0 0.1 pad_slice_fusion
  38.1 0.1 pad_maximum_fusion.4.refs_1_
  38.2 1.6 %shard_map.109 = (bf16[512,1024]{1,0:T(8,128)(2,1)S(1)}, bf16[2,480,512]{2,1,0:T(8,128)(2,1)S(1)}, bf16[2,704,256]{2,1,0:T(8,128)(2,1)S(1)}) custom-call(s32[3]{0:T(128)S(1)} %pad_add_fusion.refs_0_.meta, f32[8,128]{1,0:T(8,128)S(1)} %pad_maximum_fusion.4.refs_1_, f32[12,512]{1,0:T(8,128)S(1)} %bitcast.24, f32[22,256]{1,0:T(8,128)S(1)} %reshape.153.refs_3_), custom_call_target="tpu_custom_call" | custom-call | flops 100000000 | bytes 4194304 | tf_op jit(solution)/shard_map/pallas_call | solution.py:228
  39.8 9.3 %collective-permute-done.3.halo_up = f32[2,16,4096]{2,1,0:T(8,128)S(1)} collective-permute-done((f32[2,16,4096]{2,1,0:T(8,128)S(1)}, f32[2,16,4096]{2,1,0:T(8,128)S(1)}, u32[]{:S(2)}, u32[]{:S(2)}) %collective-permute-start.3) | collective-permute-done | bytes 524320 | tf_op jit(solution)/shard_map/ppermute | solution.py:327
  49.1 0.0 collective-permute-done.4.halo_down
  49.1 0.0 collective-permute-done.2.other
  49.1 0.0 copy-done
  49.1 23.9 %shard_map.110 = f32[2,64,4096]{2,1,0:T(8,128)} custom-call(s32[3]{0:T(128)S(1)} %pad_add_fusion.refs_0_.meta, f32[2,6]{1,0:T(2,128)S(1)} %copy-done, f32[8,96,256]{2,1,0:T(8,128)S(1)} %all-to-all-done.own, f32[8,96,256]{2,1,0:T(8,128)S(1)} %collective-permute-done.2.other, bf16[512,1024]{1,0:T(8,128)(2,1)S(1)} %get-tuple-element.18.col_weights, ...), custom_call_target="tpu_custom_call" | custom-call | flops 14000000000 | bytes 10485760 | tf_op jit(solution)/shard_map/pallas_call | solution.py:261
  (14 shorter events, 0.2 us)
Async XLA Ops:
  0.7 9.3 %collective-permute-start = (f32[16,256]{1,0:T(8,128)S(1)}, f32[16,256]{1,0:T(8,128)S(1)}, u32[]{:S(2)}, u32[]{:S(2)}) collective-permute-start(f32[16,256]{1,0:T(8,128)S(1)} %get-tuple-element.31), channel_id=1, source_target_pairs={{0,1},{1,2},{2,3},{3,4},{4,5},{5,6},{6,7},{8,9},{9,10},{10,11},{11... | collective-permute-start | bytes 49160 | tf_op jit(solution)/shard_map/ppermute | solution.py:315
  4.3 5.8 %collective-permute-start.1 = (f32[16,256]{1,0:T(8,128)S(1)}, f32[16,256]{1,0:T(8,128)S(1)}, u32[]{:S(2)}, u32[]{:S(2)}) collective-permute-start(f32[16,256]{1,0:T(8,128)S(1)} %get-tuple-element.32), channel_id=1, source_target_pairs={{1,0},{2,1},{3,2},{4,3},{5,4},{6,5},{7,6},{9,8},{10,9},{11,10},{12... | collective-permute-start | bytes 49160 | tf_op jit(solution)/shard_map/ppermute | solution.py:316
  17.9 8.4 %copy-start.2 = (s32[21]{0:T(128)S(1)}, s32[21]{0:T(128)}, u32[]{:S(2)}) copy-start(s32[21]{0:T(128)} %constant.55.clone) | copy-start | bytes 256
  17.9 18.6 %all-to-all-start = ((f32[8,96,256]{2,1,0:T(8,128)}), f32[8,96,256]{2,1,0:T(8,128)S(1)}, u32[]{:S(2)}, u32[]{:S(2)}) async-start(f32[8,96,256]{2,1,0:T(8,128)} %broadcast_in_dim.27), calls=%async_computation | async-start | bytes 1572864 | tf_op jit(solution)/shard_map/all_to_all | solution.py:363
  24.8 12.7 %copy-start.1 = (f32[2,21,6]{1,0,2:T(2,128)S(1)}, f32[2,21,6]{1,0,2:T(2,128)}, u32[]{:S(2)}) copy-start(f32[2,21,6]{1,0,2:T(2,128)} %param.15) | copy-start | bytes 3028
  26.0 23.0 %copy-start = (f32[2,6]{1,0:T(2,128)S(1)}, f32[2,6]{1,0:T(2,128)}, u32[]{:S(2)}) copy-start(f32[2,6]{1,0:T(2,128)} %back.1) | copy-start | bytes 148
  26.6 22.5 %collective-permute-start.3 = (f32[2,16,4096]{2,1,0:T(8,128)S(1)}, f32[2,16,4096]{2,1,0:T(8,128)S(1)}, u32[]{:S(2)}, u32[]{:S(2)}) collective-permute-start(f32[2,16,4096]{2,1,0:T(8,128)S(1)} %pad_maximum_fusion), channel_id=1, source_target_pairs={{0,1},{1,2},{2,3},{3,4},{4,5},{5,6},{6,7},{8,9},{9,10},{10,11},{11... | collective-permute-start | bytes 1572872 | tf_op jit(solution)/shard_map/ppermute | solution.py:327
  29.6 19.5 %collective-permute-start.4 = (f32[2,16,4096]{2,1,0:T(8,128)}, f32[2,16,4096]{2,1,0:T(8,128)S(1)}, u32[]{:S(2)}, u32[]{:S(2)}) collective-permute-start(f32[2,16,4096]{2,1,0:T(8,128)} %pad_maximum_fusion.1), channel_id=1, source_target_pairs={{1,0},{2,1},{3,2},{4,3},{5,4},{6,5},{7,6},{9,8},{10,9},{11,10},{12... | collective-permute-start | bytes 1572872 | tf_op jit(solution)/shard_map/ppermute | solution.py:328
  36.6 12.5 %collective-permute-start.2 = (f32[8,96,256]{2,1,0:T(8,128)S(1)}, f32[8,96,256]{2,1,0:T(8,128)S(1)}, u32[]{:S(2)}, u32[]{:S(2)}) collective-permute-start(f32[8,96,256]{2,1,0:T(8,128)S(1)} %all-to-all-done.own), channel_id=1, source_target_pairs={{0,8},{8,0},{16,24},{24,16},{32,40},{40,32},{48,56},{56,48},{64,72... | collective-permute-start | bytes 2359304 | tf_op jit(solution)/shard_map/ppermute | solution.py:370

commit v2 on v0

v2 whole, which is shorter than its diff:
```python
import functools

import jax
import jax.numpy as jnp
from jax import lax
from jax.experimental import pallas as pl
from jax.experimental.pallas import tpu as pltpu
from jax.sharding import PartitionSpec as P

KSIZE = 21
NBASIS = 21
NFILT = 8
NPOLY = 6
DKSIZE = 11
KHALF = 10
DHALF = 5
LANES = 128
CHUNK = 512
SHIFTS = 4
GROUPS = 3
VMEM_LIMIT = 56 * 1024 * 1024
TROWS = 96
HALFROWS = 40
MROWS = 6 * HALFROWS
KWIN = 64
DROWS = 80
F32 = jnp.float32
BF16 = jnp.bfloat16


def basis_pairs():
    basis_list = []
    for family_base, degree in ((0, 4), (5, 2)):
        for exponent in range(degree + 1):
            for second in range(degree + 1 - exponent):
                basis_list.append((family_base + exponent, family_base + second))
    return basis_list


def split(x):
    high = x.astype(BF16)
    return high, (x - high.astype(F32)).astype(BF16)


def strip_rows_norm(meta, half, strip_rows):
    rows = lax.broadcasted_iota(jnp.int32, (HALFROWS, LANES), 0) + (
        meta[0] * strip_rows - 8 + half * HALFROWS
    )
    return (2.0 * rows.astype(F32) + 1.0) / meta[2].astype(F32) - 1.0


def family_filters(widths, position):
    offsets = lax.broadcasted_iota(jnp.int32, (1, LANES), 1) - LANES // 2
    rows = []
    for family, degree in ((0, 4), (1, 2)):
        spread = 0.75 * widths[family].astype(F32)

        def profile(at):
            real = at.astype(F32)
            return jnp.where(
                jnp.abs(at) <= KHALF, jnp.exp(-(real * real) / (2.0 * spread * spread)), 0.0
            )

        current = profile(position) / jnp.sum(profile(offsets), axis=1, keepdims=True)
        scaled = position.astype(F32) / spread
        for exponent in range(degree + 1):
            rows.append(current)
            current = current * scaled
    return rows


def prepare(
    strip_rows,
    meta,
    widths,
    orders,
    coefficients,
    decor_kernel,
    col_weights,
    row_weights,
    decor_weights,
):
    visits = decor_weights.shape[0]
    lane_row = lax.broadcasted_iota(jnp.int32, (1, LANES), 1)
    filters = family_filters(widths, jnp.where(lane_row < LANES // 2, lane_row, lane_row - LANES))
    place = jnp.where(lane_row >= LANES - 2, lane_row - LANES, lane_row) + 2
    odd_place = place >= KWIN
    inner = jnp.where(odd_place, place - KWIN, place)
    windows = family_filters(widths, KHALF - inner)
    degrees = (0, 1, 1, 2, 2, 2)
    taps = {}
    for s in range(visits):
        for t in range(NPOLY):
            sums = [None] * NFILT
            for k, (row_kernel, col_kernel) in enumerate(basis_pairs()):
                weight = jnp.where(orders[k] >= degrees[t], coefficients[s, k, t], 0.0)
                term = weight * windows[row_kernel]
                sums[col_kernel] = term if sums[col_kernel] is None else sums[col_kernel] + term
            for tile in range(NFILT // 2):
                taps[s, t, tile] = jnp.where(odd_place, sums[2 * tile + 1], sums[2 * tile])
    source = lax.broadcasted_iota(jnp.int32, (LANES, LANES), 0)
    target = lax.broadcasted_iota(jnp.int32, (LANES, LANES), 1)
    near = jnp.abs(target - source) <= KHALF
    for j in range(NFILT):
        lanes = slice(j * LANES, (j + 1) * LANES)
        flat = jnp.broadcast_to(filters[j], (LANES, LANES))
        ring = pltpu.roll(flat, 0, 1, stride=1, stride_axis=0)
        high = ring.astype(BF16).astype(F32)
        low = ring - high
        col_weights[:LANES, lanes] = jnp.where(near, high, 0.0).astype(BF16)
        col_weights[LANES : 2 * LANES, lanes] = jnp.where(near, high, 0.0).astype(BF16)
        col_weights[2 * LANES : 3 * LANES, lanes] = jnp.where(near, low, 0.0).astype(BF16)
        side_high = jnp.where(near, 0.0, high)
        side_low = jnp.where(near, 0.0, low)
        packed = side_high + pltpu.roll(side_high, 20, 0) + pltpu.roll(side_low, 40, 0)
        col_weights[3 * LANES :, lanes] = packed.astype(BF16)
    for half in range(2):
        yn = strip_rows_norm(meta, half, strip_rows)
        for tile in range(4):
            parts = []
            for s in range(visits):
                rolled = []
                for t in range(NPOLY):
                    flat = jnp.broadcast_to(taps[s, t, tile], (HALFROWS, LANES))
                    rolled.append(pltpu.roll(flat, 8 * half, 1, stride=1, stride_axis=0))
                parts.append(rolled[0] + yn * (rolled[2] + yn * rolled[5]))
                parts.append(rolled[1] + yn * rolled[4])
                parts.append(rolled[3])
            high, low = split(jnp.concatenate(parts, axis=0))
            lanes = slice(tile * LANES, (tile + 1) * LANES)
            row_weights[half, :MROWS, lanes] = high
            row_weights[half, MROWS:, lanes] = low
    for s in range(visits):
        for slot in range(SHIFTS * GROUPS):
            group, shift = slot // SHIFTS, slot % SHIFTS
            rows = slice(group * strip_rows, (group + 1) * strip_rows)
            lanes = slice(shift * 2 * LANES, (shift + 1) * 2 * LANES)
            if slot < DKSIZE:
                base = jnp.zeros((1, LANES), F32)
                for tap in range(DKSIZE):
                    base = jnp.where(lane_row == DKSIZE - 1 - tap, decor_kernel[s, tap, slot], base)
                high = base.astype(BF16).astype(F32)
                low = base - high
                wide = jnp.concatenate(
                    [high + pltpu.roll(high, DROWS, 1), pltpu.roll(low, 2 * DROWS - LANES, 1)], axis=1
                )
                flat = jnp.broadcast_to(wide, (strip_rows, 2 * LANES))
                turned = pltpu.roll(flat, 3, 1, stride=1, stride_axis=0).astype(BF16)
            else:
                turned = jnp.zeros((strip_rows, 2 * LANES), BF16)
            decor_weights[s, rows, lanes] = turned


def body(
    meta,
    back,
    own,
    other,
    col_weights,
    row_weights,
    decor_weights,
    science,
    masks,
    halo_up,
    halo_down,
    out,
    high_filtered,
    low_filtered,
    diffs,
    staged,
    sent,
):
    core = meta[1]
    visits, strip_rows, col_total = science.shape
    steps = col_total // CHUNK
    chips = CHUNK // 512
    blocks_here = 4 * chips
    diffs[:, :, col_total:] = jnp.zeros((visits, DROWS, LANES), F32)
    lane = lax.broadcasted_iota(jnp.int32, (TROWS, LANES), 1)
    edge_lane = lax.broadcasted_iota(jnp.int32, (strip_rows, LANES), 1)
    low_lanes, high_lanes = slice(0, LANES), slice(LANES, 2 * LANES)

    def strip_of(chip, odd, lanes):
        return jnp.where(core == odd, own[chip, :, lanes], other[chip, :, lanes])

    def differences(step):
        slot = step % 2
        first_chip = step * chips
        last_chip = first_chip + chips
        empty = jnp.zeros((TROWS, LANES), F32)
        blocks = [strip_of(first_chip - 1, 1, high_lanes) if step else empty]
        for chip in range(first_chip, last_chip):
            for odd in range(2):
                blocks.append(strip_of(chip, odd, low_lanes))
                blocks.append(strip_of(chip, odd, high_lanes))
        blocks.append(strip_of(last_chip, 0, low_lanes) if step < steps - 1 else empty)
        stacked = []
        for b in range(blocks_here):
            high, low = split(blocks[b + 1])
            side = jnp.where(
                lane < KHALF, blocks[b + 2], jnp.where(lane >= LANES - KHALF, blocks[b], 0.0)
            )
            side_high = side.astype(BF16).astype(F32)
            side_low = side - side_high
            packed = side_high + pltpu.roll(side_low, 20, 1) + pltpu.roll(side_high, 40, 1)
            stacked.append(jnp.concatenate([high, low, high, packed.astype(BF16)], axis=1))
        lhs = jnp.concatenate(stacked, axis=0)
        for pair in range(4):
            filtered = jnp.dot(
                lhs, col_weights[:, 256 * pair : 256 * (pair + 1)], preferred_element_type=F32
            )
            for inner in range(2):
                first = (2 * pair + inner) * TROWS
                for b in range(blocks_here):
                    high, low = split(
                        filtered[TROWS * b : TROWS * (b + 1), LANES * inner : LANES * (inner + 1)]
                    )
                    high_filtered[slot, first : first + TROWS, LANES * b : LANES * (b + 1)] = high
                    low_filtered[slot, first : first + TROWS, LANES * b : LANES * (b + 1)] = low

        columns = lax.broadcasted_iota(jnp.int32, (8, CHUNK), 1) + step * CHUNK
        xn = (2.0 * columns.astype(F32) + 1.0) / float(steps * CHUNK) - 1.0
        xn = jnp.concatenate([xn] * (HALFROWS // 8), axis=0)
        start = step * CHUNK
        span = slice(start, start + CHUNK)
        for half in range(2):
            starts = [j * TROWS + 32 * half for j in range(NFILT)]
            rhs_high = [high_filtered[slot, r : r + KWIN, :] for r in starts]
            rhs_low = [low_filtered[slot, r : r + KWIN, :] for r in starts]
            wide = jnp.dot(
                row_weights[half], jnp.concatenate(rhs_high, axis=0), preferred_element_type=F32
            )
            rest = jnp.dot(
                row_weights[half, :MROWS], jnp.concatenate(rhs_low, axis=0), preferred_element_type=F32
            )
            summed = wide[:MROWS] + wide[MROWS:] + rest
            yn = strip_rows_norm(meta, half, strip_rows)[:, :1]
            for s in range(visits):
                base = s * 3 * HALFROWS
                back0 = back[s, 0] + yn * (back[s, 2] + yn * back[s, 5])
                back1 = back[s, 1] + yn * back[s, 4]
                g0 = summed[base : base + HALFROWS] + back0
                g1 = summed[base + HALFROWS : base + 2 * HALFROWS] + back1
                g2 = summed[base + 2 * HALFROWS : base + 3 * HALFROWS] + back[s, 3]
                model = g0 + xn * (g1 + xn * g2)
                rows = slice(32 * half, 32 * half + 32)
                fine = jnp.where(jnp.bitwise_and(masks[s, rows, span], 7) == 7, 0.0, 1.0)
                data, good = science[s, rows, span], fine
                blank = jnp.zeros((8 - DHALF, CHUNK), F32)
                first = (step * visits + s) * 2 * DHALF
                halo = halo_down if half else halo_up
                halo_data = halo[first : first + DHALF]
                halo_good = halo[first + DHALF : first + 2 * DHALF]
                if half == 0:
                    data = jnp.concatenate([blank, halo_data, data], axis=0)
                    good = jnp.concatenate([blank, halo_good, good], axis=0)
                else:
                    data = jnp.concatenate([data, halo_data, blank], axis=0)
                    good = jnp.concatenate([good, halo_good, blank], axis=0)
                diffs[s, half * HALFROWS : (half + 1) * HALFROWS, span] = jnp.where(
                    good > 0.5, data - model, 0.0
                )

    def shifted_products(s, window, width):
        parts = []
        for shift in range(SHIFTS):
            turned = pltpu.roll(window, width + LANES - DHALF + shift, 1)[:, :width]
            high, low = split(turned)
            parts += [high, low, high, jnp.zeros((16, width), BF16)]
        return jnp.dot(
            decor_weights[s], jnp.concatenate(parts, axis=0), preferred_element_type=F32
        )

    def left_of_patch(s):
        window = jnp.concatenate([jnp.zeros((DROWS, LANES), F32), diffs[s, :, :LANES]], axis=1)
        product = shifted_products(s, window, LANES)
        start_carry = jnp.zeros((strip_rows, LANES), F32)
        for group in range(1, GROUPS):
            shift = SHIFTS * group
            turned = pltpu.roll(product[group * strip_rows : (group + 1) * strip_rows], shift, 1)
            start_carry = start_carry + jnp.where(edge_lane < shift, turned, 0.0)
        return start_carry

    def decorrelate(step, carries):
        start = step * CHUNK
        spilled = []
        for s in range(visits):
            product = shifted_products(s, diffs[s, :, start : start + CHUNK + LANES], CHUNK)
            total = product[:strip_rows]
            to_right = jnp.zeros((strip_rows, LANES), F32)
            for group in range(1, GROUPS):
                shift = SHIFTS * group
                turned = pltpu.roll(product[group * strip_rows : (group + 1) * strip_rows], shift, 1)
                first = turned[:, :LANES]
                to_right = to_right + jnp.where(edge_lane < shift, first, 0.0)
                first = jnp.where(edge_lane < shift, 0.0, first)
                total = total + jnp.concatenate([first, turned[:, LANES:]], axis=1)
            staged[s, :, start : start + LANES] = total[:, :LANES] + carries[s]
            staged[s, :, start + LANES : start + CHUNK] = total[:, LANES:]
            spilled.append(to_right)
        return spilled

    def send(step):
        span = pl.ds(step * CHUNK, CHUNK)
        return pltpu.make_async_copy(
            staged.at[:, :, span], out.at[:, :, span], sent.at[step]
        )

    for step in range(steps):
        differences(step)
    carries = [left_of_patch(s) for s in range(visits)]
    for step in range(steps):
        carries = decorrelate(step, carries)
        send(step).start()
    for step in range(steps):
        send(step).wait()


def pack_edges(science_top, science_bottom, masks_top, masks_bottom, edge_top, edge_bottom):
    for data, bits, edge, begin in (
        (science_top, masks_top, edge_top, 0),
        (science_bottom, masks_bottom, edge_bottom, 8 - DHALF),
    ):
        rows = slice(begin, begin + DHALF)
        for s in range(data.shape[0]):
            for chunk in range(data.shape[2] // CHUNK):
                span = slice(chunk * CHUNK, (chunk + 1) * CHUNK)
                first = (chunk * data.shape[0] + s) * 2 * DHALF
                edge[first : first + DHALF] = data[s, rows, span]
                edge[first + DHALF : first + 2 * DHALF] = jnp.where(
                    jnp.bitwise_and(bits[s, rows, span], 7) == 7, 0.0, 1.0
                )


def build_edges(science, masks):
    visits, strip_rows, col_total = science.shape
    block = (visits, 8, col_total)
    top = pl.BlockSpec(block, lambda i: (0, 0, 0))
    bottom = pl.BlockSpec(block, lambda i: (0, strip_rows // 8 - 1, 0))
    edge = jax.ShapeDtypeStruct((col_total // CHUNK * visits * 2 * DHALF, CHUNK), F32)
    return pl.pallas_call(
        pack_edges,
        grid=(1,),
        out_shape=[edge, edge],
        in_specs=[top, bottom, top, bottom],
        out_specs=[whole(edge), whole(edge)],
        compiler_params=pltpu.CompilerParams(vmem_limit_bytes=VMEM_LIMIT),
        cost_estimate=pl.CostEstimate(flops=10**6, bytes_accessed=2 * 2**20, transcendentals=0),
    )(science, science, masks, masks)


def build_weights(visits, strip_rows, meta, widths, orders, coefficients, decor_kernel):
    scalar = pl.BlockSpec(memory_space=pltpu.SMEM)
    return pl.pallas_call(
        functools.partial(prepare, strip_rows),
        out_shape=[
            jax.ShapeDtypeStruct((4 * LANES, NFILT * LANES), BF16),
            jax.ShapeDtypeStruct((2, 2 * MROWS, NFILT * KWIN), BF16),
            jax.ShapeDtypeStruct((visits, GROUPS * strip_rows, SHIFTS * 2 * LANES), BF16),
        ],
        in_specs=[scalar] * 5,
        compiler_params=pltpu.CompilerParams(vmem_limit_bytes=VMEM_LIMIT),
        cost_estimate=pl.CostEstimate(flops=10**9, bytes_accessed=8 * 2**20, transcendentals=0),
    )(meta, widths, orders, coefficients, decor_kernel)


def whole(array):
    return pl.BlockSpec(array.shape, lambda i: (0,) * len(array.shape))


def fused(meta, back, templates, weights, science, masks, halo_up, halo_down):
    visits, strip_rows, col_total = science.shape
    return pl.pallas_call(
        body,
        out_shape=jax.ShapeDtypeStruct(science.shape, F32),
        in_specs=[pl.BlockSpec(memory_space=pltpu.SMEM)] * 2
        + [pl.BlockSpec(memory_space=pltpu.VMEM)] * 9,
        out_specs=pl.BlockSpec(memory_space=pl.ANY),
        scratch_shapes=[
            pltpu.VMEM((2, NFILT * TROWS, CHUNK), BF16),
            pltpu.VMEM((2, NFILT * TROWS, CHUNK), BF16),
            pltpu.VMEM((visits, DROWS, col_total + LANES), F32),
            pltpu.VMEM((visits, strip_rows, col_total), F32),
            pltpu.SemaphoreType.DMA((col_total // CHUNK,)),
        ],
        compiler_params=pltpu.CompilerParams(vmem_limit_bytes=20 * 1024 * 1024),
        cost_estimate=pl.CostEstimate(
            flops=14 * 10**9, bytes_accessed=10 * 2**20, transcendentals=0
        ),
    )(meta, back, *templates, *weights, science, masks, halo_up, halo_down)


def shards(
    science, template, gauss_widths, coeff_orders, coefficients, back_coeffs, masks, decor_kernel
):
    visits, strip_rows, col_total = science.shape
    strips = lax.axis_size("strip")
    strip = lax.axis_index("strip")
    core = lax.axis_index("visit") % 2
    up = [(i, i + 1) for i in range(strips - 1)]
    down = [(i + 1, i) for i in range(strips - 1)]

    size = lax.axis_size("visit")
    groups = [[i for i in range(size) if i % 2 == c] for c in range(2)]
    chips = size // 2
    above = lax.ppermute(template[strip_rows - 16 :], "strip", up)
    below = lax.ppermute(template[:16], "strip", down)
    edge_top, edge_bottom = build_edges(science, masks)
    above, below, edge_top, edge_bottom = lax.optimization_barrier(
        (above, below, edge_top, edge_bottom)
    )
    rimmed = jnp.concatenate([above, template, below], axis=0)
    copies = jnp.broadcast_to(rimmed[None], (chips,) + rimmed.shape)
    small = (copies, edge_top, edge_bottom, gauss_widths, coeff_orders, coefficients, decor_kernel)
    copies, edge_top, edge_bottom, *parameters = lax.optimization_barrier(small)
    own = lax.all_to_all(copies, "visit", 0, 0, axis_index_groups=groups)
    halo_up = lax.ppermute(edge_bottom, "strip", up)
    halo_down = lax.ppermute(edge_top, "strip", down)
    meta = jnp.stack([strip, core, strip_rows * strips]).astype(jnp.int32)
    weights = build_weights(visits, strip_rows, meta, *parameters)
    own, weights, halo_up, halo_down = lax.optimization_barrier((own, weights, halo_up, halo_down))
    other = lax.ppermute(own, "visit", [(i, i ^ 1) for i in range(size)])
    return fused(meta, back_coeffs, (own, other), weights, science, masks, halo_up, halo_down)


def solution(mesh):
    return jax.shard_map(
        shards,
        mesh=mesh,
        in_specs=(
            P("visit", "strip", None),
            P("strip", "visit"),
            P(),
            P(),
            P("visit", None, None),
            P("visit", None),
            P("visit", "strip", None),
            P("visit", None, None),
        ),
        out_specs=P("visit", "strip", None),
        check_vma=False,
    )
```

time: 443 us -> 63.7 us (0.14); the launches traced: 437 us -> 63 us
  matrix products: 236 us -> 0 us
  waiting for transfers between devices: 79.2 us -> 7.04 us
  local copies, waits for them, and re-layouts: 70.3 us -> 8.92 us
  Pallas kernels: 0 us -> 23 us
  other arithmetic: 21 us -> 0.56 us
  between operations: 15.2 us -> 0.08 us
  starting transfers between devices: 15.1 us -> 23.4 us
    dot_general x12 -> x0, matrix products: 236 us -> none  [the longest x6 170 us: shards(): jnp.einsum('vk,krc->vrc', effective[:, :, term], images, precision=lax.Pr...]
    all_gather x1 -> x0, waiting for transfers between devices: 76.8 us -> none  [shards(): vertical = lax.all_gather(own_filtered, 'visit', axis=2, tiled=True)]
    reshape x2 -> x0, local copies, waits for them, and re-layouts: 24.6 us -> none  [the longest x1 24.5 us: shards(): images = images.reshape(NBASIS, row_count, col_total)]
    pallas_call x0 -> x3, Pallas kernels: none -> 23 us  [the longest x1 15.5 us: fused(): pl.pallas_call(body, out_shape=jax.ShapeDtypeStruct(science.shape, F32),...]
    gather x2 -> x0, local copies, waits for them, and re-layouts: 22.5 us -> none  [the longest x1 21.9 us: shards(): blocks[row_select]]
    slice x5 -> x1, local copies, waits for them, and re-layouts: 12.5 us -> 0.74 us  [shards(): below = lax.ppermute(template[:16], 'strip', down)]
    concatenate x2 -> x1, other arithmetic: 11.2 us -> 0.01 us  [shards(): rimmed = jnp.concatenate([above, template, below], axis=0)]
    add x4 -> x0, other arithmetic: 6.81 us -> none  [the longest x1 6.78 us: shards(): result = result + padded_out[:, col_tap, :, first_col:first_col + col_total]]
  transfers between devices with their start and end apart: 5 -> 6, of which waited for: 3 -> 3; matrix products, arithmetic and copies ran while one was open for 2% -> 4% of each run, Pallas kernels for 0% -> 12%
where the time goes in v2:
time: 63.7 us; the launch traced here: 63 us
  starting transfers between devices  23.4 us (37%)
  Pallas kernels  23 us (36%)
  local copies, waits for them, and re-layouts  8.92 us (14%)
  waiting for transfers between devices  7.04 us (11%)
    pallas_call x1, Pallas kernels, fused(): pl.pallas_call(body, out_shape=jax.ShapeDtypeStruct(science.shape, F32),...  15.5 us
    all_to_all x1, starting transfers between devices, shards(): own = lax.all_to_all(copies, 'visit', 0, 0, axis_index_groups=groups)  6.7 us
    ppermute x1, starting transfers between devices, shards(): below = lax.ppermute(template[:16], 'strip', down)  5.83 us
    ppermute x1, starting transfers between devices, shards(): halo_down = lax.ppermute(edge_top, 'strip', down)  5.47 us
    pallas_call x1, Pallas kernels, build_weights(): pl.pallas_call(functools.partial(prepare, strip_rows), out_shape=[jax.Sha...  5.26 us
    unnamed x18, local copies, waits for them, and re-layouts  5.17 us
    ppermute x1, waiting for transfers between devices, shards(): halo_up = lax.ppermute(edge_bottom, 'strip', up)  2.66 us
    ppermute x1, waiting for transfers between devices, shards(): above = lax.ppermute(template[strip_rows - 16:], 'strip', up)  2.46 us
  transfers between devices with their start and end apart: 6, of which 3 were waited for; matrix products, arithmetic and copies ran while one was open for 4% of the time, Pallas kernels for 12%

profile of v2, /device:TPU:25, one launch (start us, length us, event | category | flops | bytes accessed | tf_op | source)
XLA Modules:
  0.0 63.0 jit_solution(16366588008308167065)
XLA Ops:
  0.0 0.7 %fusion = (f32[16,256]{1,0:T(8,128)S(1)}, f32[16,256]{1,0:T(8,128)S(1)}) fusion(f32[64,256]{1,0:T(8,128)} %param.9), kind=kLoop, calls=%fused_computation.2 | loop fusion | bytes 65536 | tf_op jit(solution)/shard_map/slice | solution.py:407
  0.7 5.8 %collective-permute-start.1 = (f32[16,256]{1,0:T(8,128)S(1)}, f32[16,256]{1,0:T(8,128)S(1)}, u32[]{:S(2)}, u32[]{:S(2)}) collective-permute-start(f32[16,256]{1,0:T(8,128)S(1)} %get-tuple-element.49), channel_id=1, source_target_pairs={{1,0},{2,1},{3,2},{4,3},{5,4},{6,5},{7,6},{9,8},{10,9},{11,10},{12... | collective-permute-start | bytes 49160 | tf_op jit(solution)/shard_map/ppermute | solution.py:407
  6.6 0.0 copy-start.7
  6.6 2.1 %collective-permute-start = (f32[16,256]{1,0:T(8,128)S(1)}, f32[16,256]{1,0:T(8,128)S(1)}, u32[]{:S(2)}, u32[]{:S(2)}) collective-permute-start(f32[16,256]{1,0:T(8,128)S(1)} %get-tuple-element.50), channel_id=1, source_target_pairs={{0,1},{1,2},{2,3},{3,4},{4,5},{5,6},{6,7},{8,9},{9,10},{10,11},{11... | collective-permute-start | bytes 49160 | tf_op jit(solution)/shard_map/ppermute | solution.py:406
  8.7 2.2 %shard_map.82 = (f32[160,512]{1,0:T(8,128)}, f32[160,512]{1,0:T(8,128)}) custom-call(f32[2,64,4096]{2,1,0:T(8,128)} %science.1, f32[2,64,4096]{2,1,0:T(8,128)} %science.1, s32[2,64,4096]{2,1,0:T(8,128)} %masks.1, s32[2,64,4096]{2,1,0:T(8,128)} %masks.1), custom_call_target="tpu_custom_call" | custom-call | flops 1000000 | bytes 2097152 | tf_op jit(solution)/shard_map/pallas_call | solution.py:341
  10.9 0.0 copy-start.8
  10.9 0.0 collective-permute-done.1
  10.9 2.5 %collective-permute-done = f32[16,256]{1,0:T(8,128)S(1)} collective-permute-done((f32[16,256]{1,0:T(8,128)S(1)}, f32[16,256]{1,0:T(8,128)S(1)}, u32[]{:S(2)}, u32[]{:S(2)}) %collective-permute-start) | collective-permute-done | bytes 16416 | tf_op jit(solution)/shard_map/ppermute | solution.py:406
  13.3 0.0 copy-done.7
  13.3 1.0 %broadcast_in_dim.2 = f32[8,96,256]{2,1,0:T(8,128)} broadcast(f32[96,256]{1,0:T(8,128)S(1)} %pad_maximum_fusion), dimensions={1,2} | broadcast | bytes 884736 | tf_op jit(solution)/shard_map/broadcast_in_dim | solution.py:413
  14.3 6.7 %all-to-all-start = ((f32[8,96,256]{2,1,0:T(8,128)}), f32[8,96,256]{2,1,0:T(8,128)S(1)}, u32[]{:S(2)}, u32[]{:S(2)}) async-start(f32[8,96,256]{2,1,0:T(8,128)} %broadcast_in_dim.2), calls=%async_computation | async-start | bytes 1572864 | tf_op jit(solution)/shard_map/all_to_all | solution.py:416
  21.0 0.0 copy-start
  21.0 0.0 copy-start.3
  21.0 2.0 %collective-permute-start.2 = (f32[160,512]{1,0:T(8,128)}, f32[160,512]{1,0:T(8,128)S(1)}, u32[]{:S(2)}, u32[]{:S(2)}) collective-permute-start(f32[160,512]{1,0:T(8,128)} %get-tuple-element.41), channel_id=1, source_target_pairs={{0,1},{1,2},{2,3},{3,4},{4,5},{5,6},{6,7},{8,9},{9,10},{10,11},{11... | collective-permute-start | bytes 983048 | tf_op jit(solution)/shard_map/ppermute | solution.py:417
  23.1 5.5 %collective-permute-start.3 = (f32[160,512]{1,0:T(8,128)}, f32[160,512]{1,0:T(8,128)S(1)}, u32[]{:S(2)}, u32[]{:S(2)}) collective-permute-start(f32[160,512]{1,0:T(8,128)} %get-tuple-element.42), channel_id=1, source_target_pairs={{1,0},{2,1},{3,2},{4,3},{5,4},{6,5},{7,6},{9,8},{10,9},{11,10},{12... | collective-permute-start | bytes 983048 | tf_op jit(solution)/shard_map/ppermute | solution.py:418
  28.6 0.6 pad_add_fusion.meta
  29.1 0.0 copy-start.2
  29.1 1.3 %copy.10.decor_kernel = f32[2,11,11]{2,1,0:T(8,128)} copy(f32[2,11,11]{2,0,1:T(2,128)} %param.15) | data formatting | bytes 1936 | tf_op jit(solution)/shard_map/optimization_barrier | solution.py:415
  30.4 0.0 copy-done.8
  30.5 0.7 %copy.9.coefficients = f32[2,21,6]{2,1,0:T(8,128)} copy(f32[2,21,6]{1,0,2:T(2,128)S(1)} %copy-done.8) | data formatting | bytes 2016 | tf_op jit(solution)/shard_map/optimization_barrier | solution.py:415
  31.1 5.3 %shard_map.83 = (bf16[512,1024]{1,0:T(8,128)(2,1)}, bf16[2,480,512]{2,1,0:T(8,128)(2,1)}, bf16[2,192,1024]{2,1,0:T(8,128)(2,1)}) custom-call(s32[3]{0:T(128)} %pad_add_fusion.meta, s32[2]{0:T(128)} %widths, s32[21]{0:T(128)} %orders, f32[2,21,6]{2,1,0:T(8,128)} %copy.9.coefficients, f32[2,11,11]{2,1,0:T(8,128)} %copy.10.decor_kernel), custom_call_target="tpu_custom_call" | custom-call | flops 1000000000 | bytes 8388608 | tf_op jit(solution)/shard_map/pallas_call | solution.py:354
  36.4 2.7 %collective-permute-done.2.halo_up = f32[160,512]{1,0:T(8,128)S(1)} collective-permute-done((f32[160,512]{1,0:T(8,128)}, f32[160,512]{1,0:T(8,128)S(1)}, u32[]{:S(2)}, u32[]{:S(2)}) %collective-permute-start.2) | collective-permute-done | bytes 327712 | tf_op jit(solution)/shard_map/ppermute | solution.py:417
  39.1 0.0 collective-permute-done.3.halo_down
  39.1 0.0 all-to-all-done.own
  39.1 1.3 %collective-permute-start.4 = (f32[8,96,256]{2,1,0:T(8,128)S(1)}, f32[8,96,256]{2,1,0:T(8,128)S(1)}, u32[]{:S(2)}, u32[]{:S(2)}) collective-permute-start(f32[8,96,256]{2,1,0:T(8,128)S(1)} %all-to-all-done.own), channel_id=1, source_target_pairs={{0,8},{8,0},{16,24},{24,16},{32,40},{40,32},{48,56},{56,48},{64,72... | collective-permute-start | bytes 2359304 | tf_op jit(solution)/shard_map/ppermute | solution.py:422
  40.4 1.9 %collective-permute-done.4.other = f32[8,96,256]{2,1,0:T(8,128)S(1)} collective-permute-done((f32[8,96,256]{2,1,0:T(8,128)S(1)}, f32[8,96,256]{2,1,0:T(8,128)S(1)}, u32[]{:S(2)}, u32[]{:S(2)}) %collective-permute-start.4) | collective-permute-done | bytes 786464 | tf_op jit(solution)/shard_map/ppermute | solution.py:422
  42.3 0.0 copy-done
  42.3 0.0 copy-done.3
  42.3 0.0 copy-done.2
  42.3 0.0 copy-start.1
  42.3 1.6 %copy-done.1 = s32[2,64,4096]{2,1,0:T(8,128)S(1)} copy-done((s32[2,64,4096]{2,1,0:T(8,128)S(1)}, s32[2,64,4096]{2,1,0:T(8,128)}, u32[]{:S(2)}) %copy-start.1) | copy-done | bytes 2097176
  43.9 0.0 copy-start.4
  43.9 1.2 %copy-done.4 = bf16[512,1024]{1,0:T(8,128)(2,1)S(1)} copy-done((bf16[512,1024]{1,0:T(8,128)(2,1)S(1)}, bf16[512,1024]{1,0:T(8,128)(2,1)}, u32[]{:S(2)}) %copy-start.4) | copy-done | bytes 1048600
  45.1 0.0 copy-start.5
  45.1 1.2 %copy-done.5 = bf16[2,480,512]{2,1,0:T(8,128)(2,1)S(1)} copy-done((bf16[2,480,512]{2,1,0:T(8,128)(2,1)S(1)}, bf16[2,480,512]{2,1,0:T(8,128)(2,1)}, u32[]{:S(2)}) %copy-start.5) | copy-done | bytes 983064
  46.3 0.0 copy-start.6
  46.3 1.1 %copy-done.6 = bf16[2,192,1024]{2,1,0:T(8,128)(2,1)S(1)} copy-done((bf16[2,192,1024]{2,1,0:T(8,128)(2,1)S(1)}, bf16[2,192,1024]{2,1,0:T(8,128)(2,1)}, u32[]{:S(2)}) %copy-start.6) | copy-done | bytes 786456
  47.4 15.5 %shard_map.84 = f32[2,64,4096]{2,1,0:T(8,128)} custom-call(s32[3]{0:T(128)S(1)} %copy-done.2, f32[2,6]{1,0:T(2,128)S(1)} %copy-done.3, f32[8,96,256]{2,1,0:T(8,128)S(1)} %all-to-all-done.own, f32[8,96,256]{2,1,0:T(8,128)S(1)} %collective-permute-done.4.other, bf16[512,1024]{1,0:T(8,128)(2,1)S(1)} %copy-done.4, bf16[2,480,512]{2,1,0:T(8,128)(2,1)S(1)} %copy-done.5, ...), custom_call_target="tpu_custom_call" | custom-call | flops 14000000000 | bytes 10485760 | tf_op jit(solution)/shard_map/pallas_call | solution.py:373
  (1 shorter events, 0.0 us)
Async XLA Ops:
  0.7 10.1 %collective-permute-start.1 = (f32[16,256]{1,0:T(8,128)S(1)}, f32[16,256]{1,0:T(8,128)S(1)}, u32[]{:S(2)}, u32[]{:S(2)}) collective-permute-start(f32[16,256]{1,0:T(8,128)S(1)} %get-tuple-element.49), channel_id=1, source_target_pairs={{1,0},{2,1},{3,2},{4,3},{5,4},{6,5},{7,6},{9,8},{10,9},{11,10},{12... | collective-permute-start | bytes 49160 | tf_op jit(solution)/shard_map/ppermute | solution.py:407
  6.6 6.7 %copy-start.7 = (f32[64,256]{1,0:T(8,128)S(1)}, f32[64,256]{1,0:T(8,128)}, u32[]{:S(2)}) copy-start(f32[64,256]{1,0:T(8,128)} %param.9) | copy-start | bytes 196612
  6.6 6.7 %collective-permute-start = (f32[16,256]{1,0:T(8,128)S(1)}, f32[16,256]{1,0:T(8,128)S(1)}, u32[]{:S(2)}, u32[]{:S(2)}) collective-permute-start(f32[16,256]{1,0:T(8,128)S(1)} %get-tuple-element.50), channel_id=1, source_target_pairs={{0,1},{1,2},{2,3},{3,4},{4,5},{5,6},{6,7},{8,9},{9,10},{10,11},{11... | collective-permute-start | bytes 49160 | tf_op jit(solution)/shard_map/ppermute | solution.py:406
  10.9 19.6 %copy-start.8 = (f32[2,21,6]{1,0,2:T(2,128)S(1)}, f32[2,21,6]{1,0,2:T(2,128)}, u32[]{:S(2)}) copy-start(f32[2,21,6]{1,0,2:T(2,128)} %param.12) | copy-start | bytes 3028
  14.3 24.7 %all-to-all-start = ((f32[8,96,256]{2,1,0:T(8,128)}), f32[8,96,256]{2,1,0:T(8,128)S(1)}, u32[]{:S(2)}, u32[]{:S(2)}) async-start(f32[8,96,256]{2,1,0:T(8,128)} %broadcast_in_dim.2), calls=%async_computation | async-start | bytes 1572864 | tf_op jit(solution)/shard_map/all_to_all | solution.py:416
  21.0 21.2 %copy-start = (f32[2,64,4096]{2,1,0:T(8,128)S(1)}, f32[2,64,4096]{2,1,0:T(8,128)}, u32[]{:S(2)}) copy-start(f32[2,64,4096]{2,1,0:T(8,128)} %science.1) | copy-start | bytes 6291460
  21.0 21.2 %copy-start.3 = (f32[2,6]{1,0:T(2,128)S(1)}, f32[2,6]{1,0:T(2,128)}, u32[]{:S(2)}) copy-start(f32[2,6]{1,0:T(2,128)} %back.1) | copy-start | bytes 148
  21.0 18.0 %collective-permute-start.2 = (f32[160,512]{1,0:T(8,128)}, f32[160,512]{1,0:T(8,128)S(1)}, u32[]{:S(2)}, u32[]{:S(2)}) collective-permute-start(f32[160,512]{1,0:T(8,128)} %get-tuple-element.41), channel_id=1, source_target_pairs={{0,1},{1,2},{2,3},{3,4},{4,5},{5,6},{6,7},{8,9},{9,10},{10,11},{11... | collective-permute-start | bytes 983048 | tf_op jit(solution)/shard_map/ppermute | solution.py:417
  23.1 16.0 %collective-permute-start.3 = (f32[160,512]{1,0:T(8,128)}, f32[160,512]{1,0:T(8,128)S(1)}, u32[]{:S(2)}, u32[]{:S(2)}) collective-permute-start(f32[160,512]{1,0:T(8,128)} %get-tuple-element.42), channel_id=1, source_target_pairs={{1,0},{2,1},{3,2},{4,3},{5,4},{6,5},{7,6},{9,8},{10,9},{11,10},{12... | collective-permute-start | bytes 983048 | tf_op jit(solution)/shard_map/ppermute | solution.py:418
  29.1 13.1 %copy-start.2 = (s32[3]{0:T(128)S(1)}, s32[3]{0:T(128)}, u32[]{:S(2)}) copy-start(s32[3]{0:T(128)} %pad_add_fusion.meta) | copy-start | bytes 40
  39.1 3.2 %collective-permute-start.4 = (f32[8,96,256]{2,1,0:T(8,128)S(1)}, f32[8,96,256]{2,1,0:T(8,128)S(1)}, u32[]{:S(2)}, u32[]{:S(2)}) collective-permute-start(f32[8,96,256]{2,1,0:T(8,128)S(1)} %all-to-all-done.own), channel_id=1, source_target_pairs={{0,8},{8,0},{16,24},{24,16},{32,40},{40,32},{48,56},{56,48},{64,72... | collective-permute-start | bytes 2359304 | tf_op jit(solution)/shard_map/ppermute | solution.py:422
  42.3 1.6 %copy-start.1 = (s32[2,64,4096]{2,1,0:T(8,128)S(1)}, s32[2,64,4096]{2,1,0:T(8,128)}, u32[]{:S(2)}) copy-start(s32[2,64,4096]{2,1,0:T(8,128)} %masks.1) | copy-start | bytes 6291460
  43.9 1.2 %copy-start.4 = (bf16[512,1024]{1,0:T(8,128)(2,1)S(1)}, bf16[512,1024]{1,0:T(8,128)(2,1)}, u32[]{:S(2)}) copy-start(bf16[512,1024]{1,0:T(8,128)(2,1)} %get-tuple-element.44.col_weights) | copy-start | bytes 3145732
  45.1 1.2 %copy-start.5 = (bf16[2,480,512]{2,1,0:T(8,128)(2,1)S(1)}, bf16[2,480,512]{2,1,0:T(8,128)(2,1)}, u32[]{:S(2)}) copy-start(bf16[2,480,512]{2,1,0:T(8,128)(2,1)} %get-tuple-element.45.row_weights) | copy-start | bytes 2949124
  46.3 1.1 %copy-start.6 = (bf16[2,192,1024]{2,1,0:T(8,128)(2,1)S(1)}, bf16[2,192,1024]{2,1,0:T(8,128)(2,1)}, u32[]{:S(2)}) copy-start(bf16[2,192,1024]{2,1,0:T(8,128)(2,1)} %get-tuple-element.46.decor_weights) | copy-start | bytes 2359300

commit v3 on v2

--- a/solution.py
+++ b/solution.py
@@ -79,7 +79,9 @@
     col_weights,
     row_weights,
     decor_weights,
+    token,
 ):
+    token[...] = jnp.zeros_like(token)
     visits = decor_weights.shape[0]
     lane_row = lax.broadcasted_iota(jnp.int32, (1, LANES), 1)
     filters = family_filters(widths, jnp.where(lane_row < LANES // 2, lane_row, lane_row - LANES))
@@ -154,13 +156,14 @@
 def body(
     meta,
     back,
+    token,
     own,
     other,
-    col_weights,
-    row_weights,
-    decor_weights,
+    col_source,
+    row_source,
+    decor_source,
     science,
-    masks,
+    masks_source,
     halo_up,
     halo_down,
     out,
@@ -168,8 +171,26 @@
     low_filtered,
     diffs,
     staged,
+    col_weights,
+    row_weights,
+    decor_weights,
+    masks,
     sent,
+    arrived,
 ):
+    fetches = [
+        pltpu.make_async_copy(source, copy, arrived.at[index])
+        for index, (source, copy) in enumerate(
+            (
+                (col_source, col_weights),
+                (row_source, row_weights),
+                (masks_source, masks),
+                (decor_source, decor_weights),
+            )
+        )
+    ]
+    fetches[0].start()
+    fetches[1].start()
     core = meta[1]
     visits, strip_rows, col_total = science.shape
     steps = col_total // CHUNK
@@ -218,6 +239,8 @@
                     high_filtered[slot, first : first + TROWS, LANES * b : LANES * (b + 1)] = high
                     low_filtered[slot, first : first + TROWS, LANES * b : LANES * (b + 1)] = low
 
+        if step == 0:
+            fetches[1].wait()
         columns = lax.broadcasted_iota(jnp.int32, (8, CHUNK), 1) + step * CHUNK
         xn = (2.0 * columns.astype(F32) + 1.0) / float(steps * CHUNK) - 1.0
         xn = jnp.concatenate([xn] * (HALFROWS // 8), axis=0)
@@ -234,6 +257,8 @@
                 row_weights[half, :MROWS], jnp.concatenate(rhs_low, axis=0), preferred_element_type=F32
             )
             summed = wide[:MROWS] + wide[MROWS:] + rest
+            if step == 0 and half == 0:
+                fetches[2].wait()
             yn = strip_rows_norm(meta, half, strip_rows)[:, :1]
             for s in range(visits):
                 base = s * 3 * HALFROWS
@@ -306,8 +331,12 @@
             staged.at[:, :, span], out.at[:, :, span], sent.at[step]
         )
 
+    fetches[0].wait()
+    fetches[2].start()
+    fetches[3].start()
     for step in range(steps):
         differences(step)
+    fetches[3].wait()
     carries = [left_of_patch(s) for s in range(visits)]
     for step in range(steps):
         carries = decorrelate(step, carries)
@@ -357,6 +386,7 @@
             jax.ShapeDtypeStruct((4 * LANES, NFILT * LANES), BF16),
             jax.ShapeDtypeStruct((2, 2 * MROWS, NFILT * KWIN), BF16),
             jax.ShapeDtypeStruct((visits, GROUPS * strip_rows, SHIFTS * 2 * LANES), BF16),
+            jax.ShapeDtypeStruct((8, LANES), F32),
         ],
         in_specs=[scalar] * 5,
         compiler_params=pltpu.CompilerParams(vmem_limit_bytes=VMEM_LIMIT),
@@ -368,26 +398,33 @@
     return pl.BlockSpec(array.shape, lambda i: (0,) * len(array.shape))
 
 
-def fused(meta, back, templates, weights, science, masks, halo_up, halo_down):
+def fused(meta, back, token, templates, weights, science, masks, halo_up, halo_down):
     visits, strip_rows, col_total = science.shape
     return pl.pallas_call(
         body,
         out_shape=jax.ShapeDtypeStruct(science.shape, F32),
         in_specs=[pl.BlockSpec(memory_space=pltpu.SMEM)] * 2
-        + [pl.BlockSpec(memory_space=pltpu.VMEM)] * 9,
+        + [pl.BlockSpec(memory_space=pl.ANY)]
+        + [pl.BlockSpec(memory_space=pltpu.VMEM)] * 2
+        + [pl.BlockSpec(memory_space=pl.ANY)] * 3
+        + [pl.BlockSpec(memory_space=pltpu.VMEM)]
+        + [pl.BlockSpec(memory_space=pl.ANY)]
+        + [pl.BlockSpec(memory_space=pltpu.VMEM)] * 2,
         out_specs=pl.BlockSpec(memory_space=pl.ANY),
         scratch_shapes=[
             pltpu.VMEM((2, NFILT * TROWS, CHUNK), BF16),
             pltpu.VMEM((2, NFILT * TROWS, CHUNK), BF16),
             pltpu.VMEM((visits, DROWS, col_total + LANES), F32),
             pltpu.VMEM((visits, strip_rows, col_total), F32),
+            *[pltpu.VMEM(array.shape, array.dtype) for array in (*weights, masks)],
             pltpu.SemaphoreType.DMA((col_total // CHUNK,)),
+            pltpu.SemaphoreType.DMA((4,)),
         ],
-        compiler_params=pltpu.CompilerParams(vmem_limit_bytes=20 * 1024 * 1024),
+        compiler_params=pltpu.CompilerParams(vmem_limit_bytes=VMEM_LIMIT),
         cost_estimate=pl.CostEstimate(
             flops=14 * 10**9, bytes_accessed=10 * 2**20, transcendentals=0
         ),
-    )(meta, back, *templates, *weights, science, masks, halo_up, halo_down)
+    )(meta, back, token, *templates, *weights, science, masks, halo_up, halo_down)
 
 
 def shards(
@@ -417,10 +454,10 @@
     halo_up = lax.ppermute(edge_bottom, "strip", up)
     halo_down = lax.ppermute(edge_top, "strip", down)
     meta = jnp.stack([strip, core, strip_rows * strips]).astype(jnp.int32)
-    weights = build_weights(visits, strip_rows, meta, *parameters)
-    own, weights, halo_up, halo_down = lax.optimization_barrier((own, weights, halo_up, halo_down))
+    *weights, token = build_weights(visits, strip_rows, meta, *parameters)
+    own, token, halo_up, halo_down = lax.optimization_barrier((own, token, halo_up, halo_down))
     other = lax.ppermute(own, "visit", [(i, i ^ 1) for i in range(size)])
-    return fused(meta, back_coeffs, (own, other), weights, science, masks, halo_up, halo_down)
+    return fused(meta, back_coeffs, token, (own, other), weights, science, masks, halo_up, halo_down)
 
 
 def solution(mesh):

time: 63.7 us -> 67.2 us (1.055)
  Pallas kernels: 23 us -> 30.5 us
  local copies, waits for them, and re-layouts: 8.92 us -> 3.9 us
  waiting for transfers between devices: 7.04 us -> 7.91 us
    pallas_call x1, Pallas kernels: 15.5 us -> 23.1 us  [fused(): pl.pallas_call(body, out_shape=jax.ShapeDtypeStruct(science.shape, F32),...]
    unnamed x18, local copies, waits for them, and re-layouts: 5.17 us -> 0.91 us
    ppermute x1, waiting for transfers between devices: 2.66 us -> 3.55 us  [shards(): halo_up = lax.ppermute(edge_bottom, 'strip', up)]
    optimization_barrier x2, local copies, waits for them, and re-layouts: 2 us -> 1.31 us  [shards(): copies, edge_top, edge_bottom, *parameters = lax.optimization_barrier(small)]
  transfers between devices with their start and end apart: 6 -> 6, of which waited for: 3 -> 3; matrix products, arithmetic and copies ran while one was open for 4% -> 3% of each run, Pallas kernels for 12% -> 11%
where the time goes in v3:
time: 67.2 us; the launch traced here: 66.6 us
  Pallas kernels  30.5 us (45%)
  starting transfers between devices  23.4 us (35%)
  waiting for transfers between devices  7.91 us (12%)
  local copies, waits for them, and re-layouts  3.9 us (6%)
    pallas_call x1, Pallas kernels, fused(): pl.pallas_call(body, out_shape=jax.ShapeDtypeStruct(science.shape, F32),...  23.1 us
    all_to_all x1, starting transfers between devices, shards(): own = lax.all_to_all(copies, 'visit', 0, 0, axis_index_groups=groups)  6.7 us
    ppermute x1, starting transfers between devices, shards(): below = lax.ppermute(template[:16], 'strip', down)  5.83 us
    ppermute x1, starting transfers between devices, shards(): halo_down = lax.ppermute(edge_top, 'strip', down)  5.47 us
    pallas_call x1, Pallas kernels, build_weights(): pl.pallas_call(functools.partial(prepare, strip_rows), out_shape=[jax.Sha...  5.26 us
    ppermute x1, waiting for transfers between devices, shards(): halo_up = lax.ppermute(edge_bottom, 'strip', up)  3.55 us
    ppermute x1, waiting for transfers between devices, shards(): above = lax.ppermute(template[strip_rows - 16:], 'strip', up)  2.44 us
    pallas_call x1, Pallas kernels, build_edges(): pl.pallas_call(pack_edges, grid=(1,), out_shape=[edge, edge], in_specs=[t...  2.19 us
  transfers between devices with their start and end apart: 6, of which 3 were waited for; matrix products, arithmetic and copies ran while one was open for 3% of the time, Pallas kernels for 11%

profile of v3, /device:TPU:25, one launch (start us, length us, event | category | flops | bytes accessed | tf_op | source)
XLA Modules:
  0.0 66.6 jit_solution(4074168896872622836)
XLA Ops:
  0.0 0.7 %fusion = (f32[16,256]{1,0:T(8,128)S(1)}, f32[16,256]{1,0:T(8,128)S(1)}) fusion(f32[64,256]{1,0:T(8,128)} %param.9), kind=kLoop, calls=%fused_computation.2 | loop fusion | bytes 65536 | tf_op jit(solution)/shard_map/slice | solution.py:444
  0.7 5.8 %collective-permute-start.1 = (f32[16,256]{1,0:T(8,128)S(1)}, f32[16,256]{1,0:T(8,128)S(1)}, u32[]{:S(2)}, u32[]{:S(2)}) collective-permute-start(f32[16,256]{1,0:T(8,128)S(1)} %get-tuple-element.47), channel_id=1, source_target_pairs={{1,0},{2,1},{3,2},{4,3},{5,4},{6,5},{7,6},{9,8},{10,9},{11,10},{12... | collective-permute-start | bytes 49160 | tf_op jit(solution)/shard_map/ppermute | solution.py:444
  6.6 0.0 copy-start.1
  6.6 2.1 %collective-permute-start = (f32[16,256]{1,0:T(8,128)S(1)}, f32[16,256]{1,0:T(8,128)S(1)}, u32[]{:S(2)}, u32[]{:S(2)}) collective-permute-start(f32[16,256]{1,0:T(8,128)S(1)} %get-tuple-element.48), channel_id=1, source_target_pairs={{0,1},{1,2},{2,3},{3,4},{4,5},{5,6},{6,7},{8,9},{9,10},{10,11},{11... | collective-permute-start | bytes 49160 | tf_op jit(solution)/shard_map/ppermute | solution.py:443
  8.7 2.2 %shard_map.82 = (f32[160,512]{1,0:T(8,128)}, f32[160,512]{1,0:T(8,128)}) custom-call(f32[2,64,4096]{2,1,0:T(8,128)} %science.1, f32[2,64,4096]{2,1,0:T(8,128)} %science.1, s32[2,64,4096]{2,1,0:T(8,128)} %masks_source.1, s32[2,64,4096]{2,1,0:T(8,128)} %masks_source.1), custom_call_target="tpu_custom_call" | custom-call | flops 1000000 | bytes 2097152 | tf_op jit(solution)/shard_map/pallas_call | solution.py:370
  10.8 0.0 copy-start.6
  10.8 0.0 copy-start.5
  10.8 0.0 copy-start.2
  10.9 0.0 copy-start.3
  10.9 0.0 collective-permute-done.1
  10.9 2.4 %collective-permute-done = f32[16,256]{1,0:T(8,128)S(1)} collective-permute-done((f32[16,256]{1,0:T(8,128)S(1)}, f32[16,256]{1,0:T(8,128)S(1)}, u32[]{:S(2)}, u32[]{:S(2)}) %collective-permute-start) | collective-permute-done | bytes 16416 | tf_op jit(solution)/shard_map/ppermute | solution.py:443
  13.3 0.0 copy-done.1
  13.3 0.9 %broadcast_in_dim.2 = f32[8,96,256]{2,1,0:T(8,128)} broadcast(f32[96,256]{1,0:T(8,128)S(1)} %pad_maximum_fusion), dimensions={1,2} | broadcast | bytes 884736 | tf_op jit(solution)/shard_map/broadcast_in_dim | solution.py:450
  14.3 6.7 %all-to-all-start = ((f32[8,96,256]{2,1,0:T(8,128)}), f32[8,96,256]{2,1,0:T(8,128)S(1)}, u32[]{:S(2)}, u32[]{:S(2)}) async-start(f32[8,96,256]{2,1,0:T(8,128)} %broadcast_in_dim.2), calls=%async_computation | async-start | bytes 1572864 | tf_op jit(solution)/shard_map/all_to_all | solution.py:453
  21.0 0.0 copy-done.6
  21.0 1.9 %collective-permute-start.2 = (f32[160,512]{1,0:T(8,128)S(1)}, f32[160,512]{1,0:T(8,128)S(1)}, u32[]{:S(2)}, u32[]{:S(2)}) collective-permute-start(f32[160,512]{1,0:T(8,128)S(1)} %copy-done.6), channel_id=1, source_target_pairs={{0,1},{1,2},{2,3},{3,4},{4,5},{5,6},{6,7},{8,9},{9,10},{10,11},{11... | collective-permute-start | bytes 983048 | tf_op jit(solution)/shard_map/ppermute | solution.py:454
  22.9 0.0 copy-done.5
  22.9 5.5 %collective-permute-start.3 = (f32[160,512]{1,0:T(8,128)S(1)}, f32[160,512]{1,0:T(8,128)S(1)}, u32[]{:S(2)}, u32[]{:S(2)}) collective-permute-start(f32[160,512]{1,0:T(8,128)S(1)} %copy-done.5), channel_id=1, source_target_pairs={{1,0},{2,1},{3,2},{4,3},{5,4},{6,5},{7,6},{9,8},{10,9},{11,10},{12... | collective-permute-start | bytes 983048 | tf_op jit(solution)/shard_map/ppermute | solution.py:455
  28.4 0.6 pad_add_fusion.meta
  29.0 0.0 copy-done.2
  29.0 0.6 copy.10.decor_kernel
  29.6 0.0 copy-done.3
  29.6 0.7 %copy.9.coefficients = f32[2,21,6]{2,1,0:T(8,128)} copy(f32[2,21,6]{1,0,2:T(2,128)S(1)} %copy-done.3) | data formatting | bytes 2016 | tf_op jit(solution)/shard_map/optimization_barrier | solution.py:452
  30.3 5.3 %shard_map.83 = (bf16[512,1024]{1,0:T(8,128)(2,1)}, bf16[2,480,512]{2,1,0:T(8,128)(2,1)}, bf16[2,192,1024]{2,1,0:T(8,128)(2,1)}, f32[8,128]{1,0:T(8,128)}) custom-call(s32[3]{0:T(128)} %pad_add_fusion.meta, s32[2]{0:T(128)} %widths, s32[21]{0:T(128)} %orders, f32[2,21,6]{2,1,0:T(8,128)} %copy.9.coefficients, f32[2,11,11]{2,1,0:T(8,128)} %copy.10.decor_kernel), custom_call_target="tpu_custom_call" | custom-call | flops 1000000000 | bytes 8388608 | tf_op jit(solution)/shard_map/pallas_call | solution.py:383
  35.6 3.5 %collective-permute-done.2.halo_up = f32[160,512]{1,0:T(8,128)S(1)} collective-permute-done((f32[160,512]{1,0:T(8,128)S(1)}, f32[160,512]{1,0:T(8,128)S(1)}, u32[]{:S(2)}, u32[]{:S(2)}) %collective-permute-start.2) | collective-permute-done | bytes 327712 | tf_op jit(solution)/shard_map/ppermute | solution.py:454
  39.1 0.0 copy-start.7
  39.1 0.0 collective-permute-done.3.halo_down
  39.1 0.0 copy-start.8
  39.1 0.0 all-to-all-done.own
  39.1 0.0 copy-start
  39.2 1.4 %collective-permute-start.4 = (f32[8,96,256]{2,1,0:T(8,128)S(1)}, f32[8,96,256]{2,1,0:T(8,128)S(1)}, u32[]{:S(2)}, u32[]{:S(2)}) collective-permute-start(f32[8,96,256]{2,1,0:T(8,128)S(1)} %all-to-all-done.own), channel_id=1, source_target_pairs={{0,8},{8,0},{16,24},{24,16},{32,40},{40,32},{48,56},{56,48},{64,72... | collective-permute-start | bytes 2359304 | tf_op jit(solution)/shard_map/ppermute | solution.py:459
  40.6 1.9 %collective-permute-done.4.other = f32[8,96,256]{2,1,0:T(8,128)S(1)} collective-permute-done((f32[8,96,256]{2,1,0:T(8,128)S(1)}, f32[8,96,256]{2,1,0:T(8,128)S(1)}, u32[]{:S(2)}, u32[]{:S(2)}) %collective-permute-start.4) | collective-permute-done | bytes 786464 | tf_op jit(solution)/shard_map/ppermute | solution.py:459
  42.5 0.0 copy-start.4
  42.5 0.0 copy-done.7
  42.5 0.0 copy-done.8
  42.5 0.0 copy-done
  42.5 0.9 %copy-done.4 = f32[8,96,256]{2,1,0:T(8,128)} copy-done((f32[8,96,256]{2,1,0:T(8,128)}, f32[8,96,256]{2,1,0:T(8,128)S(1)}, u32[]{:S(2)}) %copy-start.4) | copy-done | bytes 786456
  43.4 23.1 %shard_map.84 = f32[2,64,4096]{2,1,0:T(8,128)} custom-call(s32[3]{0:T(128)} %pad_add_fusion.meta, f32[2,6]{1,0:T(2,128)} %back.1, f32[8,128]{1,0:T(8,128)} %get-tuple-element.40.token, f32[8,96,256]{2,1,0:T(8,128)} %copy-done, f32[8,96,256]{2,1,0:T(8,128)} %copy-done.4, bf16[512,1024]{1,0:T(8,128)(2,1)} %get-tuple-element.42.col_source, ...), custom_call_target="tpu_custom_call" | custom-call | flops 14000000000 | bytes 10485760 | tf_op jit(solution)/shard_map/pallas_call | solution.py:403
  (1 shorter events, 0.0 us)
Async XLA Ops:
  0.7 10.1 %collective-permute-start.1 = (f32[16,256]{1,0:T(8,128)S(1)}, f32[16,256]{1,0:T(8,128)S(1)}, u32[]{:S(2)}, u32[]{:S(2)}) collective-permute-start(f32[16,256]{1,0:T(8,128)S(1)} %get-tuple-element.47), channel_id=1, source_target_pairs={{1,0},{2,1},{3,2},{4,3},{5,4},{6,5},{7,6},{9,8},{10,9},{11,10},{12... | collective-permute-start | bytes 49160 | tf_op jit(solution)/shard_map/ppermute | solution.py:444
  6.6 6.7 %copy-start.1 = (f32[64,256]{1,0:T(8,128)S(1)}, f32[64,256]{1,0:T(8,128)}, u32[]{:S(2)}) copy-start(f32[64,256]{1,0:T(8,128)} %param.9) | copy-start | bytes 196612
  6.6 6.7 %collective-permute-start = (f32[16,256]{1,0:T(8,128)S(1)}, f32[16,256]{1,0:T(8,128)S(1)}, u32[]{:S(2)}, u32[]{:S(2)}) collective-permute-start(f32[16,256]{1,0:T(8,128)S(1)} %get-tuple-element.48), channel_id=1, source_target_pairs={{0,1},{1,2},{2,3},{3,4},{4,5},{5,6},{6,7},{8,9},{9,10},{10,11},{11... | collective-permute-start | bytes 49160 | tf_op jit(solution)/shard_map/ppermute | solution.py:443
  10.8 10.1 %copy-start.6 = (f32[160,512]{1,0:T(8,128)S(1)}, f32[160,512]{1,0:T(8,128)}, u32[]{:S(2)}) copy-start(f32[160,512]{1,0:T(8,128)} %get-tuple-element.38) | copy-start | bytes 983044
  10.8 12.1 %copy-start.5 = (f32[160,512]{1,0:T(8,128)S(1)}, f32[160,512]{1,0:T(8,128)}, u32[]{:S(2)}) copy-start(f32[160,512]{1,0:T(8,128)} %get-tuple-element.39) | copy-start | bytes 983044
  10.8 18.2 %copy-start.2 = (f32[2,11,11]{2,0,1:T(2,128)S(1)}, f32[2,11,11]{2,0,1:T(2,128)}, u32[]{:S(2)}) copy-start(f32[2,11,11]{2,0,1:T(2,128)} %param.15) | copy-start | bytes 2908
  10.9 18.8 %copy-start.3 = (f32[2,21,6]{1,0,2:T(2,128)S(1)}, f32[2,21,6]{1,0,2:T(2,128)}, u32[]{:S(2)}) copy-start(f32[2,21,6]{1,0,2:T(2,128)} %param.12) | copy-start | bytes 3028
  14.3 24.9 %all-to-all-start = ((f32[8,96,256]{2,1,0:T(8,128)}), f32[8,96,256]{2,1,0:T(8,128)S(1)}, u32[]{:S(2)}, u32[]{:S(2)}) async-start(f32[8,96,256]{2,1,0:T(8,128)} %broadcast_in_dim.2), calls=%async_computation | async-start | bytes 1572864 | tf_op jit(solution)/shard_map/all_to_all | solution.py:453
  21.0 18.1 %collective-permute-start.2 = (f32[160,512]{1,0:T(8,128)S(1)}, f32[160,512]{1,0:T(8,128)S(1)}, u32[]{:S(2)}, u32[]{:S(2)}) collective-permute-start(f32[160,512]{1,0:T(8,128)S(1)} %copy-done.6), channel_id=1, source_target_pairs={{0,1},{1,2},{2,3},{3,4},{4,5},{5,6},{6,7},{8,9},{9,10},{10,11},{11... | collective-permute-start | bytes 983048 | tf_op jit(solution)/shard_map/ppermute | solution.py:454
  22.9 16.2 %collective-permute-start.3 = (f32[160,512]{1,0:T(8,128)S(1)}, f32[160,512]{1,0:T(8,128)S(1)}, u32[]{:S(2)}, u32[]{:S(2)}) collective-permute-start(f32[160,512]{1,0:T(8,128)S(1)} %copy-done.5), channel_id=1, source_target_pairs={{1,0},{2,1},{3,2},{4,3},{5,4},{6,5},{7,6},{9,8},{10,9},{11,10},{12... | collective-permute-start | bytes 983048 | tf_op jit(solution)/shard_map/ppermute | solution.py:455
  39.1 3.4 %copy-start.7 = (f32[160,512]{1,0:T(8,128)}, f32[160,512]{1,0:T(8,128)S(1)}, u32[]{:S(2)}) copy-start(f32[160,512]{1,0:T(8,128)S(1)} %collective-permute-done.2.halo_up) | copy-start | bytes 983044
  39.1 3.4 %copy-start.8 = (f32[160,512]{1,0:T(8,128)}, f32[160,512]{1,0:T(8,128)S(1)}, u32[]{:S(2)}) copy-start(f32[160,512]{1,0:T(8,128)S(1)} %collective-permute-done.3.halo_down) | copy-start | bytes 983044
  39.1 3.4 %copy-start = (f32[8,96,256]{2,1,0:T(8,128)}, f32[8,96,256]{2,1,0:T(8,128)S(1)}, u32[]{:S(2)}) copy-start(f32[8,96,256]{2,1,0:T(8,128)S(1)} %all-to-all-done.own) | copy-start | bytes 2359300
  39.2 3.4 %collective-permute-start.4 = (f32[8,96,256]{2,1,0:T(8,128)S(1)}, f32[8,96,256]{2,1,0:T(8,128)S(1)}, u32[]{:S(2)}, u32[]{:S(2)}) collective-permute-start(f32[8,96,256]{2,1,0:T(8,128)S(1)} %all-to-all-done.own), channel_id=1, source_target_pairs={{0,8},{8,0},{16,24},{24,16},{32,40},{40,32},{48,56},{56,48},{64,72... | collective-permute-start | bytes 2359304 | tf_op jit(solution)/shard_map/ppermute | solution.py:459
  42.5 0.9 %copy-start.4 = (f32[8,96,256]{2,1,0:T(8,128)}, f32[8,96,256]{2,1,0:T(8,128)S(1)}, u32[]{:S(2)}) copy-start(f32[8,96,256]{2,1,0:T(8,128)S(1)} %collective-permute-done.4.other) | copy-start | bytes 2359300

commit v4 on v2

--- a/solution.py
+++ b/solution.py
@@ -76,11 +76,12 @@
     orders,
     coefficients,
     decor_kernel,
-    col_weights,
-    row_weights,
-    decor_weights,
+    weights,
 ):
-    visits = decor_weights.shape[0]
+    visits = coefficients.shape[0]
+    col_weights = weights.at[: 4 * LANES]
+    row_weights = weights.at[4 * LANES : 4 * LANES + 2 * MROWS]
+    decor_weights = weights.at[4 * LANES + 2 * MROWS :]
     lane_row = lax.broadcasted_iota(jnp.int32, (1, LANES), 1)
     filters = family_filters(widths, jnp.where(lane_row < LANES // 2, lane_row, lane_row - LANES))
     place = jnp.where(lane_row >= LANES - 2, lane_row - LANES, lane_row) + 2
@@ -127,13 +128,14 @@
                 parts.append(rolled[1] + yn * rolled[4])
                 parts.append(rolled[3])
             high, low = split(jnp.concatenate(parts, axis=0))
-            lanes = slice(tile * LANES, (tile + 1) * LANES)
-            row_weights[half, :MROWS, lanes] = high
-            row_weights[half, MROWS:, lanes] = low
+            first = half * NFILT * KWIN + tile * LANES
+            row_weights[:MROWS, first : first + LANES] = high
+            row_weights[MROWS:, first : first + LANES] = low
     for s in range(visits):
         for slot in range(SHIFTS * GROUPS):
             group, shift = slot // SHIFTS, slot % SHIFTS
-            rows = slice(group * strip_rows, (group + 1) * strip_rows)
+            first = (s * GROUPS + group) * strip_rows
+            rows = slice(first, first + strip_rows)
             lanes = slice(shift * 2 * LANES, (shift + 1) * 2 * LANES)
             if slot < DKSIZE:
                 base = jnp.zeros((1, LANES), F32)
@@ -148,7 +150,7 @@
                 turned = pltpu.roll(flat, 3, 1, stride=1, stride_axis=0).astype(BF16)
             else:
                 turned = jnp.zeros((strip_rows, 2 * LANES), BF16)
-            decor_weights[s, rows, lanes] = turned
+            decor_weights[rows, lanes] = turned
 
 
 def body(
@@ -156,9 +158,7 @@
     back,
     own,
     other,
-    col_weights,
-    row_weights,
-    decor_weights,
+    weights,
     science,
     masks,
     halo_up,
@@ -207,7 +207,7 @@
         lhs = jnp.concatenate(stacked, axis=0)
         for pair in range(4):
             filtered = jnp.dot(
-                lhs, col_weights[:, 256 * pair : 256 * (pair + 1)], preferred_element_type=F32
+                lhs, weights[: 4 * LANES, 256 * pair : 256 * (pair + 1)], preferred_element_type=F32
             )
             for inner in range(2):
                 first = (2 * pair + inner) * TROWS
@@ -227,11 +227,13 @@
             starts = [j * TROWS + 32 * half for j in range(NFILT)]
             rhs_high = [high_filtered[slot, r : r + KWIN, :] for r in starts]
             rhs_low = [low_filtered[slot, r : r + KWIN, :] for r in starts]
+            row_first = 4 * LANES
+            row_lanes = slice(half * NFILT * KWIN, (half + 1) * NFILT * KWIN)
             wide = jnp.dot(
-                row_weights[half], jnp.concatenate(rhs_high, axis=0), preferred_element_type=F32
+                weights[row_first : row_first + 2 * MROWS, row_lanes], jnp.concatenate(rhs_high, axis=0), preferred_element_type=F32
             )
             rest = jnp.dot(
-                row_weights[half, :MROWS], jnp.concatenate(rhs_low, axis=0), preferred_element_type=F32
+                weights[row_first : row_first + MROWS, row_lanes], jnp.concatenate(rhs_low, axis=0), preferred_element_type=F32
             )
             summed = wide[:MROWS] + wide[MROWS:] + rest
             yn = strip_rows_norm(meta, half, strip_rows)[:, :1]
@@ -267,8 +269,9 @@
             turned = pltpu.roll(window, width + LANES - DHALF + shift, 1)[:, :width]
             high, low = split(turned)
             parts += [high, low, high, jnp.zeros((16, width), BF16)]
+        first = 4 * LANES + 2 * MROWS + s * GROUPS * strip_rows
         return jnp.dot(
-            decor_weights[s], jnp.concatenate(parts, axis=0), preferred_element_type=F32
+            weights[first : first + GROUPS * strip_rows], jnp.concatenate(parts, axis=0), preferred_element_type=F32
         )
 
     def left_of_patch(s):
@@ -353,11 +356,9 @@
     scalar = pl.BlockSpec(memory_space=pltpu.SMEM)
     return pl.pallas_call(
         functools.partial(prepare, strip_rows),
-        out_shape=[
-            jax.ShapeDtypeStruct((4 * LANES, NFILT * LANES), BF16),
-            jax.ShapeDtypeStruct((2, 2 * MROWS, NFILT * KWIN), BF16),
-            jax.ShapeDtypeStruct((visits, GROUPS * strip_rows, SHIFTS * 2 * LANES), BF16),
-        ],
+        out_shape=jax.ShapeDtypeStruct(
+            (4 * LANES + 2 * MROWS + visits * GROUPS * strip_rows, NFILT * LANES), BF16
+        ),
         in_specs=[scalar] * 5,
         compiler_params=pltpu.CompilerParams(vmem_limit_bytes=VMEM_LIMIT),
         cost_estimate=pl.CostEstimate(flops=10**9, bytes_accessed=8 * 2**20, transcendentals=0),
@@ -374,7 +375,7 @@
         body,
         out_shape=jax.ShapeDtypeStruct(science.shape, F32),
         in_specs=[pl.BlockSpec(memory_space=pltpu.SMEM)] * 2
-        + [pl.BlockSpec(memory_space=pltpu.VMEM)] * 9,
+        + [pl.BlockSpec(memory_space=pltpu.VMEM)] * 7,
         out_specs=pl.BlockSpec(memory_space=pl.ANY),
         scratch_shapes=[
             pltpu.VMEM((2, NFILT * TROWS, CHUNK), BF16),
@@ -387,7 +388,7 @@
         cost_estimate=pl.CostEstimate(
             flops=14 * 10**9, bytes_accessed=10 * 2**20, transcendentals=0
         ),
-    )(meta, back, *templates, *weights, science, masks, halo_up, halo_down)
+    )(meta, back, *templates, weights, science, masks, halo_up, halo_down)
 
 
 def shards(

time: 63.7 us -> 61.7 us (0.969)
  local copies, waits for them, and re-layouts: 8.92 us -> 7.09 us
    unnamed x18 -> x14, local copies, waits for them, and re-layouts: 5.17 us -> 3.4 us
where the time goes in v4:
time: 61.7 us; the launch traced here: 61.2 us
  starting transfers between devices  23.4 us (38%)
  Pallas kernels  23.1 us (37%)
  local copies, waits for them, and re-layouts  7.09 us (11%)
  waiting for transfers between devices  6.92 us (11%)
    pallas_call x1, Pallas kernels, fused(): pl.pallas_call(body, out_shape=jax.ShapeDtypeStruct(science.shape, F32),...  15.5 us
    all_to_all x1, starting transfers between devices, shards(): own = lax.all_to_all(copies, 'visit', 0, 0, axis_index_groups=groups)  6.7 us
    ppermute x1, starting transfers between devices, shards(): below = lax.ppermute(template[:16], 'strip', down)  5.83 us
    ppermute x1, starting transfers between devices, shards(): halo_down = lax.ppermute(edge_top, 'strip', down)  5.47 us
    pallas_call x1, Pallas kernels, build_weights(): pl.pallas_call(functools.partial(prepare, strip_rows), out_shape=jax.Shap...  5.33 us
    unnamed x14, local copies, waits for them, and re-layouts  3.4 us
    ppermute x1, waiting for transfers between devices, shards(): halo_up = lax.ppermute(edge_bottom, 'strip', up)  2.54 us
    ppermute x1, waiting for transfers between devices, shards(): above = lax.ppermute(template[strip_rows - 16:], 'strip', up)  2.46 us
  transfers between devices with their start and end apart: 6, of which 3 were waited for; matrix products, arithmetic and copies ran while one was open for 4% of the time, Pallas kernels for 12%

profile of v4, /device:TPU:25, one launch (start us, length us, event | category | flops | bytes accessed | tf_op | source)
XLA Modules:
  0.0 61.2 jit_solution(14681263742914661820)
XLA Ops:
  0.0 0.7 %fusion = (f32[16,256]{1,0:T(8,128)S(1)}, f32[16,256]{1,0:T(8,128)S(1)}) fusion(f32[64,256]{1,0:T(8,128)} %param.9), kind=kLoop, calls=%fused_computation.2 | loop fusion | bytes 65536 | tf_op jit(solution)/shard_map/slice | solution.py:408
  0.7 5.8 %collective-permute-start.1 = (f32[16,256]{1,0:T(8,128)S(1)}, f32[16,256]{1,0:T(8,128)S(1)}, u32[]{:S(2)}, u32[]{:S(2)}) collective-permute-start(f32[16,256]{1,0:T(8,128)S(1)} %get-tuple-element.39), channel_id=1, source_target_pairs={{1,0},{2,1},{3,2},{4,3},{5,4},{6,5},{7,6},{9,8},{10,9},{11,10},{12... | collective-permute-start | bytes 49160 | tf_op jit(solution)/shard_map/ppermute | solution.py:408
  6.6 0.0 copy-start.5
  6.6 2.1 %collective-permute-start = (f32[16,256]{1,0:T(8,128)S(1)}, f32[16,256]{1,0:T(8,128)S(1)}, u32[]{:S(2)}, u32[]{:S(2)}) collective-permute-start(f32[16,256]{1,0:T(8,128)S(1)} %get-tuple-element.40), channel_id=1, source_target_pairs={{0,1},{1,2},{2,3},{3,4},{4,5},{5,6},{6,7},{8,9},{9,10},{10,11},{11... | collective-permute-start | bytes 49160 | tf_op jit(solution)/shard_map/ppermute | solution.py:407
  8.7 2.2 %shard_map.82 = (f32[160,512]{1,0:T(8,128)}, f32[160,512]{1,0:T(8,128)}) custom-call(f32[2,64,4096]{2,1,0:T(8,128)} %science.1, f32[2,64,4096]{2,1,0:T(8,128)} %science.1, s32[2,64,4096]{2,1,0:T(8,128)} %masks.1, s32[2,64,4096]{2,1,0:T(8,128)} %masks.1), custom_call_target="tpu_custom_call" | custom-call | flops 1000000 | bytes 2097152 | tf_op jit(solution)/shard_map/pallas_call | solution.py:344
  10.9 0.0 copy-start.6
  10.9 0.0 collective-permute-done.1
  10.9 2.5 %collective-permute-done = f32[16,256]{1,0:T(8,128)S(1)} collective-permute-done((f32[16,256]{1,0:T(8,128)S(1)}, f32[16,256]{1,0:T(8,128)S(1)}, u32[]{:S(2)}, u32[]{:S(2)}) %collective-permute-start) | collective-permute-done | bytes 16416 | tf_op jit(solution)/shard_map/ppermute | solution.py:407
  13.3 0.0 copy-done.5
  13.3 0.9 %broadcast_in_dim.2 = f32[8,96,256]{2,1,0:T(8,128)} broadcast(f32[96,256]{1,0:T(8,128)S(1)} %pad_maximum_fusion), dimensions={1,2} | broadcast | bytes 884736 | tf_op jit(solution)/shard_map/broadcast_in_dim | solution.py:414
  14.3 6.7 %all-to-all-start = ((f32[8,96,256]{2,1,0:T(8,128)}), f32[8,96,256]{2,1,0:T(8,128)S(1)}, u32[]{:S(2)}, u32[]{:S(2)}) async-start(f32[8,96,256]{2,1,0:T(8,128)} %broadcast_in_dim.2), calls=%async_computation | async-start | bytes 1572864 | tf_op jit(solution)/shard_map/all_to_all | solution.py:417
  21.0 0.0 copy-start
  21.0 0.0 copy-start.3
  21.0 2.0 %collective-permute-start.2 = (f32[160,512]{1,0:T(8,128)}, f32[160,512]{1,0:T(8,128)S(1)}, u32[]{:S(2)}, u32[]{:S(2)}) collective-permute-start(f32[160,512]{1,0:T(8,128)} %get-tuple-element.33), channel_id=1, source_target_pairs={{0,1},{1,2},{2,3},{3,4},{4,5},{5,6},{6,7},{8,9},{9,10},{10,11},{11... | collective-permute-start | bytes 983048 | tf_op jit(solution)/shard_map/ppermute | solution.py:418
  23.0 5.5 %collective-permute-start.3 = (f32[160,512]{1,0:T(8,128)}, f32[160,512]{1,0:T(8,128)S(1)}, u32[]{:S(2)}, u32[]{:S(2)}) collective-permute-start(f32[160,512]{1,0:T(8,128)} %get-tuple-element.34), channel_id=1, source_target_pairs={{1,0},{2,1},{3,2},{4,3},{5,4},{6,5},{7,6},{9,8},{10,9},{11,10},{12... | collective-permute-start | bytes 983048 | tf_op jit(solution)/shard_map/ppermute | solution.py:419
  28.5 0.6 pad_add_fusion.meta
  29.1 0.0 copy-start.2
  29.1 1.3 %copy.10.decor_kernel = f32[2,11,11]{2,1,0:T(8,128)} copy(f32[2,11,11]{2,0,1:T(2,128)} %param.15) | data formatting | bytes 1936 | tf_op jit(solution)/shard_map/optimization_barrier | solution.py:416
  30.4 0.0 copy-done.6
  30.4 0.7 %copy.9.coefficients = f32[2,21,6]{2,1,0:T(8,128)} copy(f32[2,21,6]{1,0,2:T(2,128)S(1)} %copy-done.6) | data formatting | bytes 2016 | tf_op jit(solution)/shard_map/optimization_barrier | solution.py:416
  31.1 5.3 %shard_map.83.weights = bf16[1376,1024]{1,0:T(8,128)(2,1)} custom-call(s32[3]{0:T(128)} %pad_add_fusion.meta, s32[2]{0:T(128)} %widths, s32[21]{0:T(128)} %orders, f32[2,21,6]{2,1,0:T(8,128)} %copy.9.coefficients, f32[2,11,11]{2,1,0:T(8,128)} %copy.10.decor_kernel), custom_call_target="tpu_custom_call" | custom-call | flops 1000000000 | bytes 8388608 | tf_op jit(solution)/shard_map/pallas_call | solution.py:357
  36.5 2.5 %collective-permute-done.2.halo_up = f32[160,512]{1,0:T(8,128)S(1)} collective-permute-done((f32[160,512]{1,0:T(8,128)}, f32[160,512]{1,0:T(8,128)S(1)}, u32[]{:S(2)}, u32[]{:S(2)}) %collective-permute-start.2) | collective-permute-done | bytes 327712 | tf_op jit(solution)/shard_map/ppermute | solution.py:418
  39.0 0.0 collective-permute-done.3.halo_down
  39.0 0.0 all-to-all-done.own
  39.0 1.3 %collective-permute-start.4 = (f32[8,96,256]{2,1,0:T(8,128)S(1)}, f32[8,96,256]{2,1,0:T(8,128)S(1)}, u32[]{:S(2)}, u32[]{:S(2)}) collective-permute-start(f32[8,96,256]{2,1,0:T(8,128)S(1)} %all-to-all-done.own), channel_id=1, source_target_pairs={{0,8},{8,0},{16,24},{24,16},{32,40},{40,32},{48,56},{56,48},{64,72... | collective-permute-start | bytes 2359304 | tf_op jit(solution)/shard_map/ppermute | solution.py:423
  40.3 1.9 %collective-permute-done.4.other = f32[8,96,256]{2,1,0:T(8,128)S(1)} collective-permute-done((f32[8,96,256]{2,1,0:T(8,128)S(1)}, f32[8,96,256]{2,1,0:T(8,128)S(1)}, u32[]{:S(2)}, u32[]{:S(2)}) %collective-permute-start.4) | collective-permute-done | bytes 786464 | tf_op jit(solution)/shard_map/ppermute | solution.py:423
  42.2 0.0 copy-done
  42.2 0.0 copy-done.3
  42.2 0.0 copy-done.2
  42.2 0.0 copy-start.1
  42.2 1.6 %copy-done.1 = s32[2,64,4096]{2,1,0:T(8,128)S(1)} copy-done((s32[2,64,4096]{2,1,0:T(8,128)S(1)}, s32[2,64,4096]{2,1,0:T(8,128)}, u32[]{:S(2)}) %copy-start.1) | copy-done | bytes 2097176
  43.8 0.0 copy-start.4
  43.8 1.8 %copy-done.4 = bf16[1376,1024]{1,0:T(8,128)(2,1)S(1)} copy-done((bf16[1376,1024]{1,0:T(8,128)(2,1)S(1)}, bf16[1376,1024]{1,0:T(8,128)(2,1)}, u32[]{:S(2)}) %copy-start.4) | copy-done | bytes 2818072
  45.6 15.5 %shard_map.84 = f32[2,64,4096]{2,1,0:T(8,128)} custom-call(s32[3]{0:T(128)S(1)} %copy-done.2, f32[2,6]{1,0:T(2,128)S(1)} %copy-done.3, f32[8,96,256]{2,1,0:T(8,128)S(1)} %all-to-all-done.own, f32[8,96,256]{2,1,0:T(8,128)S(1)} %collective-permute-done.4.other, bf16[1376,1024]{1,0:T(8,128)(2,1)S(1)} %copy-done.4, f32[2,64,4096]{2,1,0:T(8,128)S(1)} %copy-done, ...), custom_call_target="tpu_custom_call" | custom-call | flops 14000000000 | bytes 10485760 | tf_op jit(solution)/shard_map/pallas_call | solution.py:374
  (1 shorter events, 0.0 us)
Async XLA Ops:
  0.7 10.1 %collective-permute-start.1 = (f32[16,256]{1,0:T(8,128)S(1)}, f32[16,256]{1,0:T(8,128)S(1)}, u32[]{:S(2)}, u32[]{:S(2)}) collective-permute-start(f32[16,256]{1,0:T(8,128)S(1)} %get-tuple-element.39), channel_id=1, source_target_pairs={{1,0},{2,1},{3,2},{4,3},{5,4},{6,5},{7,6},{9,8},{10,9},{11,10},{12... | collective-permute-start | bytes 49160 | tf_op jit(solution)/shard_map/ppermute | solution.py:408
  6.6 6.7 %copy-start.5 = (f32[64,256]{1,0:T(8,128)S(1)}, f32[64,256]{1,0:T(8,128)}, u32[]{:S(2)}) copy-start(f32[64,256]{1,0:T(8,128)} %param.9) | copy-start | bytes 196612
  6.6 6.7 %collective-permute-start = (f32[16,256]{1,0:T(8,128)S(1)}, f32[16,256]{1,0:T(8,128)S(1)}, u32[]{:S(2)}, u32[]{:S(2)}) collective-permute-start(f32[16,256]{1,0:T(8,128)S(1)} %get-tuple-element.40), channel_id=1, source_target_pairs={{0,1},{1,2},{2,3},{3,4},{4,5},{5,6},{6,7},{8,9},{9,10},{10,11},{11... | collective-permute-start | bytes 49160 | tf_op jit(solution)/shard_map/ppermute | solution.py:407
  10.9 19.6 %copy-start.6 = (f32[2,21,6]{1,0,2:T(2,128)S(1)}, f32[2,21,6]{1,0,2:T(2,128)}, u32[]{:S(2)}) copy-start(f32[2,21,6]{1,0,2:T(2,128)} %param.12) | copy-start | bytes 3028
  14.3 24.7 %all-to-all-start = ((f32[8,96,256]{2,1,0:T(8,128)}), f32[8,96,256]{2,1,0:T(8,128)S(1)}, u32[]{:S(2)}, u32[]{:S(2)}) async-start(f32[8,96,256]{2,1,0:T(8,128)} %broadcast_in_dim.2), calls=%async_computation | async-start | bytes 1572864 | tf_op jit(solution)/shard_map/all_to_all | solution.py:417
  21.0 21.2 %copy-start = (f32[2,64,4096]{2,1,0:T(8,128)S(1)}, f32[2,64,4096]{2,1,0:T(8,128)}, u32[]{:S(2)}) copy-start(f32[2,64,4096]{2,1,0:T(8,128)} %science.1) | copy-start | bytes 6291460
  21.0 21.2 %copy-start.3 = (f32[2,6]{1,0:T(2,128)S(1)}, f32[2,6]{1,0:T(2,128)}, u32[]{:S(2)}) copy-start(f32[2,6]{1,0:T(2,128)} %back.1) | copy-start | bytes 148
  21.0 18.0 %collective-permute-start.2 = (f32[160,512]{1,0:T(8,128)}, f32[160,512]{1,0:T(8,128)S(1)}, u32[]{:S(2)}, u32[]{:S(2)}) collective-permute-start(f32[160,512]{1,0:T(8,128)} %get-tuple-element.33), channel_id=1, source_target_pairs={{0,1},{1,2},{2,3},{3,4},{4,5},{5,6},{6,7},{8,9},{9,10},{10,11},{11... | collective-permute-start | bytes 983048 | tf_op jit(solution)/shard_map/ppermute | solution.py:418
  23.0 16.0 %collective-permute-start.3 = (f32[160,512]{1,0:T(8,128)}, f32[160,512]{1,0:T(8,128)S(1)}, u32[]{:S(2)}, u32[]{:S(2)}) collective-permute-start(f32[160,512]{1,0:T(8,128)} %get-tuple-element.34), channel_id=1, source_target_pairs={{1,0},{2,1},{3,2},{4,3},{5,4},{6,5},{7,6},{9,8},{10,9},{11,10},{12... | collective-permute-start | bytes 983048 | tf_op jit(solution)/shard_map/ppermute | solution.py:419
  29.1 13.1 %copy-start.2 = (s32[3]{0:T(128)S(1)}, s32[3]{0:T(128)}, u32[]{:S(2)}) copy-start(s32[3]{0:T(128)} %pad_add_fusion.meta) | copy-start | bytes 40
  39.0 3.2 %collective-permute-start.4 = (f32[8,96,256]{2,1,0:T(8,128)S(1)}, f32[8,96,256]{2,1,0:T(8,128)S(1)}, u32[]{:S(2)}, u32[]{:S(2)}) collective-permute-start(f32[8,96,256]{2,1,0:T(8,128)S(1)} %all-to-all-done.own), channel_id=1, source_target_pairs={{0,8},{8,0},{16,24},{24,16},{32,40},{40,32},{48,56},{56,48},{64,72... | collective-permute-start | bytes 2359304 | tf_op jit(solution)/shard_map/ppermute | solution.py:423
  42.2 1.6 %copy-start.1 = (s32[2,64,4096]{2,1,0:T(8,128)S(1)}, s32[2,64,4096]{2,1,0:T(8,128)}, u32[]{:S(2)}) copy-start(s32[2,64,4096]{2,1,0:T(8,128)} %masks.1) | copy-start | bytes 6291460
  43.8 1.8 %copy-start.4 = (bf16[1376,1024]{1,0:T(8,128)(2,1)S(1)}, bf16[1376,1024]{1,0:T(8,128)(2,1)}, u32[]{:S(2)}) copy-start(bf16[1376,1024]{1,0:T(8,128)(2,1)} %shard_map.83.weights) | copy-start | bytes 8454148
